TPU v7x, 256 devices: a whole 4x4x8 slice. The times are simulated.
256 devices in a mesh: blk: 32 (over z_hi, y, x), tm: 8 (over z_lo, core).
Axes of the slice: x: 4, y: 4, z: 8 (z_hi: 2, z_lo: 4; z = z_hi * 4 + z_lo), core: 2. Of those that a mesh axis runs over, the one named last changes fastest.
Arguments:
- returns: bfloat16 [16384, 2048], P('blk', 'tm'), may hold values from -6 to 6
- plan: int32 [2, 32], replicated, may hold values from 0 to 31, as said below
- pair_mask: int32 [32, 32], replicated, may hold values 0 or 1
Outputs:
- lead_lag: bfloat16 [16384, 2, 7680], P(('blk', 'tm'))
Inputs may be any that keep to these rules, and one draw needn't show every extreme that they name: Each round r has a word m_r with plan[r, b] = b XOR m_r for every block b; m_r is never 0, and every bit of a block index is set in the word of some round.
All inputs are finite; a program needn't handle non-finite values.
Results may differ from a plain program's by a relative error of at most 0.001.
Values may be sent and summed in bfloat16 or wider, within the bound.
No kernel may reach another device: no remote copies, remote signals or barrier semaphores. Data moves between devices by JAX's collectives and lax.ppermute only.
A program may use at most 64 MiB of HBM per device.

v0:
```python
import jax
import jax.numpy as jnp
from jax import lax
from jax.sharding import Mesh
from jax.sharding import PartitionSpec as P

LAG = 7
ROUNDS = 2
TM = ("tm_0", "tm_1")
BLK_TM = ("blk", "tm_0", "tm_1")


def swapped(block, axis, stride):
    count = lax.axis_size(axis)
    route = []
    for low in range(count):
        high = low | 1 << stride
        if high != low and high < count:
            route += [(low, high), (high, low)]
    return lax.ppermute(block, axis, route)


def cut_along(shard, dim, size):
    shape = shard.shape
    blocks = shard.reshape(*shape[:dim], size, shape[dim] // size, *shape[dim + 1 :])
    return jnp.moveaxis(blocks, dim, 0)


def in_order(blocks, dim):
    shape = list(blocks.shape[1:])
    shape[dim] *= blocks.shape[0]
    return jnp.moveaxis(blocks, 0, dim).reshape(shape)


def exchange_in_order(blocks, axes, sequence):
    shape = [lax.axis_size(a) for a in axes]
    blocks = blocks.reshape(*shape, *blocks.shape[1:])
    for k in sequence:
        blocks = lax.all_to_all(blocks, axes[k], split_axis=k, concat_axis=k, tiled=True)
    return blocks.reshape(-1, *blocks.shape[len(axes) :])


def exchange_by_chip(shard, groups, sequence, split_dim, concat_dim):
    size = lax.axis_size(groups[0]) * lax.axis_size(groups[1])
    blocks = cut_along(shard, split_dim, size)
    return in_order(exchange_in_order(blocks, groups, sequence), concat_dim)


def on_device(returns, plan, pair_mask):
    own_block = lax.axis_index("blk")
    bit_count = lax.axis_size("blk").bit_length() - 1
    slab_count = lax.axis_size(TM)
    minutes = returns.shape[1]
    minutes_all = minutes * slab_count
    factor = float(minutes_all) ** (-0.5)
    collected = []
    own_part = exchange_by_chip(returns, ("tm_0", "tm_1"), (1, 0), 0, 1)
    row_count = own_part.shape[0]
    own_padded = jnp.pad(own_part, ((0, 0), (LAG, LAG)))
    own_shifted = jnp.stack(
        [
            lax.slice_in_dim(own_padded, 2 * LAG - offset, 2 * LAG - offset + minutes_all, axis=1)
            for offset in range(2 * LAG + 1)
        ],
        axis=0,
    )
    for round_id in range(ROUNDS):
        mask_word = plan[round_id, 0]
        partner = jnp.bitwise_xor(own_block, mask_word)
        pair_live = pair_mask[own_block, partner]
        current = returns
        for bit in range(bit_count):
            flag = jnp.bitwise_and(jnp.right_shift(mask_word, bit), 1)
            current = lax.cond(
                flag == 1, lambda value: swapped(value, "blk", bit), lambda value: value, current
            )
        gathered = lax.all_gather(current, TM, axis=1, tiled=True)
        tiles = lax.dot_general(
            own_shifted, gathered, (((2,), (1,)), ((), ())), preferred_element_type=jnp.float32
        )
        gram = jnp.transpose(tiles, (1, 0, 2)).reshape(row_count, -1)
        collected.append(gram * (factor * pair_live.astype(jnp.float32)))
    return jnp.stack(collected, axis=1).astype(jnp.bfloat16)


def solution(mesh):
    split = Mesh(mesh.devices.reshape(mesh.shape["blk"], 4, 2), ("blk", "tm_0", "tm_1"))
    return jax.shard_map(
        on_device,
        mesh=split,
        in_specs=(P("blk", TM), P(), P()),
        out_specs=P(BLK_TM, None, None),
        check_vma=False,
    )
```

profile of v0, /device:TPU:1, one launch (start us, length us, event | category | flops | bytes accessed | tf_op | source)
XLA Modules:
  0.0 137.7 jit_solution(110807131863328362)
XLA Ops:
  6.5 1.4 fusion.15
  11.0 1.7 %conditional.10 = (bf16[512,256]{1,0:T(8,128)(2,1)}) conditional(s32[]{:T(128)} %convert_element_type.45, bf16[512,256]{1,0:T(8,128)(2,1)} %param.23, bf16[512,256]{1,0:T(8,128)(2,1)} %param.23), branch_computations={%region_0.1_spmd, %region_1.2_spmd} | conditional | bytes 1048624 | solution.py:74
  11.0 1.7 %copy.44 = bf16[512,256]{1,0:T(8,128)(2,1)} copy(bf16[512,256]{1,0:T(8,128)(2,1)} %param) | data formatting | bytes 524288 | tf_op jit(solution)/shard_map/cond
  12.7 9.6 %conditional.11 = (bf16[512,256]{1,0:T(8,128)(2,1)}) conditional(s32[]{:T(128)} %convert_element_type.44, bf16[512,256]{1,0:T(8,128)(2,1)} %get-tuple-element.59, bf16[512,256]{1,0:T(8,128)(2,1)} %get-tuple-element.59), branch_computations={%region_2.3_spmd, %region_3.4_spmd} | conditional | bytes 1572912 | solution.py:74
  12.7 3.6 %collective-permute-start.1 = (bf16[512,256]{1,0:T(8,128)(2,1)}, bf16[512,256]{1,0:T(8,128)(2,1)S(1)}, u32[]{:S(2)}, u32[]{:S(2)}) collective-permute-start(bf16[512,256]{1,0:T(8,128)(2,1)} %param.3), channel_id=1, source_target_pairs={{0,16},{16,0},{8,24},{24,8},{32,48},{48,32},{40,56},{56,40},{64,80... | collective-permute-start | bytes 786440 | tf_op jit(solution)/shard_map/cond/branch_1_fun/ppermute | solution.py:20
  16.2 5.3 %collective-permute-done.1 = bf16[512,256]{1,0:T(8,128)(2,1)S(1)} collective-permute-done((bf16[512,256]{1,0:T(8,128)(2,1)}, bf16[512,256]{1,0:T(8,128)(2,1)S(1)}, u32[]{:S(2)}, u32[]{:S(2)}) %collective-permute-start.1) | collective-permute-done | bytes 262176 | tf_op jit(solution)/shard_map/cond/branch_1_fun/ppermute | solution.py:20
  23.2 6.0 %all_to_all.10 = bf16[4,2,64,256]{3,2,0,1:T(8,128)(2,1)S(1)} all-to-all(bf16[4,2,64,256]{3,2,0,1:T(8,128)(2,1)S(1)} %copy.12), channel_id=1, replica_groups=mesh['blk'=32,'tm_0'=4,'tm_1'=2] {'tm_1'}, dimensions={1} | all-to-all | bytes 524288 | tf_op jit(solution)/shard_map/all_to_all | solution.py:39
  30.0 5.6 %all-to-all-start.1 = ((bf16[4,2,64,256]{3,2,1,0:T(8,128)(2,1)}), bf16[4,2,64,256]{3,2,1,0:T(8,128)(2,1)S(1)}, u32[]{:S(2)}, u32[]{:S(2)}) async-start(bf16[4,2,64,256]{3,2,1,0:T(8,128)(2,1)} %copy.13), calls=%async_computation.1 | async-start | bytes 524288 | tf_op jit(solution)/shard_map/all_to_all | solution.py:39
  39.0 7.4 %conditional.15 = (bf16[512,256]{1,0:T(8,128)(2,1)}) conditional(s32[]{:T(128)} %convert_element_type.51, bf16[512,256]{1,0:T(8,128)(2,1)S(1)} %copy-done, bf16[512,256]{1,0:T(8,128)(2,1)S(1)} %copy-done), branch_computations={%region_10.11_spmd, %region_11.12_spmd} | conditional | bytes 1048624 | solution.py:74
  39.0 1.3 collective-permute-start.5
  40.3 6.1 %collective-permute-done.5 = bf16[512,256]{1,0:T(8,128)(2,1)} collective-permute-done((bf16[512,256]{1,0:T(8,128)(2,1)S(1)}, bf16[512,256]{1,0:T(8,128)(2,1)}, u32[]{:S(2)}, u32[]{:S(2)}) %collective-permute-start.5) | collective-permute-done | bytes 262176 | tf_op jit(solution)/shard_map/cond/branch_1_fun/ppermute | solution.py:20
  46.5 7.2 %conditional.17 = (bf16[512,256]{1,0:T(8,128)(2,1)}) conditional(s32[]{:T(128)} %convert_element_type.49, bf16[512,256]{1,0:T(8,128)(2,1)} %get-tuple-element.65, bf16[512,256]{1,0:T(8,128)(2,1)} %get-tuple-element.65), branch_computations={%region_14.15_spmd, %region_15.16_spmd} | conditional | bytes 1572912 | solution.py:74
  47.8 5.2 %collective-permute-done.7 = bf16[512,256]{1,0:T(8,128)(2,1)S(1)} collective-permute-done((bf16[512,256]{1,0:T(8,128)(2,1)}, bf16[512,256]{1,0:T(8,128)(2,1)S(1)}, u32[]{:S(2)}, u32[]{:S(2)}) %collective-permute-start.7) | collective-permute-done | bytes 262176 | tf_op jit(solution)/shard_map/cond/branch_1_fun/ppermute | solution.py:20
  53.7 7.9 %conditional.18 = (bf16[512,256]{1,0:T(8,128)(2,1)}) conditional(s32[]{:T(128)} %convert_element_type.48, bf16[512,256]{1,0:T(8,128)(2,1)} %get-tuple-element.66, bf16[512,256]{1,0:T(8,128)(2,1)} %get-tuple-element.66), branch_computations={%region_16.17_spmd, %region_17.18_spmd} | conditional | bytes 1572912 | solution.py:74
  53.7 2.9 %collective-permute-start.8 = (bf16[512,256]{1,0:T(8,128)(2,1)}, bf16[512,256]{1,0:T(8,128)(2,1)S(1)}, u32[]{:S(2)}, u32[]{:S(2)}) collective-permute-start(bf16[512,256]{1,0:T(8,128)(2,1)} %param.17), channel_id=1, source_target_pairs={{0,64},{64,0},{8,72},{72,8},{16,80},{80,16},{24,88},{88,24},{32,96... | collective-permute-start | bytes 786440 | tf_op jit(solution)/shard_map/cond/branch_1_fun/ppermute | solution.py:20
  56.6 4.3 %collective-permute-done.8 = bf16[512,256]{1,0:T(8,128)(2,1)S(1)} collective-permute-done((bf16[512,256]{1,0:T(8,128)(2,1)}, bf16[512,256]{1,0:T(8,128)(2,1)S(1)}, u32[]{:S(2)}, u32[]{:S(2)}) %collective-permute-start.8) | collective-permute-done | bytes 262176 | tf_op jit(solution)/shard_map/cond/branch_1_fun/ppermute | solution.py:20
  61.6 14.4 %conditional.19 = (bf16[512,256]{1,0:T(8,128)(2,1)}) conditional(s32[]{:T(128)} %convert_element_type.47, bf16[512,256]{1,0:T(8,128)(2,1)} %get-tuple-element.67, bf16[512,256]{1,0:T(8,128)(2,1)} %get-tuple-element.67), branch_computations={%region_18.19_spmd, %region_19.20_spmd} | conditional | bytes 1572912 | solution.py:74
  61.6 5.6 %collective-permute-start.9 = (bf16[512,256]{1,0:T(8,128)(2,1)}, bf16[512,256]{1,0:T(8,128)(2,1)S(1)}, u32[]{:S(2)}, u32[]{:S(2)}) collective-permute-start(bf16[512,256]{1,0:T(8,128)(2,1)} %param.19), channel_id=1, source_target_pairs={{0,128},{128,0},{8,136},{136,8},{16,144},{144,16},{24,152},{152,24... | collective-permute-start | bytes 786440 | tf_op jit(solution)/shard_map/cond/branch_1_fun/ppermute | solution.py:20
  67.2 8.1 %collective-permute-done.9 = bf16[512,256]{1,0:T(8,128)(2,1)S(1)} collective-permute-done((bf16[512,256]{1,0:T(8,128)(2,1)}, bf16[512,256]{1,0:T(8,128)(2,1)S(1)}, u32[]{:S(2)}, u32[]{:S(2)}) %collective-permute-start.9) | collective-permute-done | bytes 262176 | tf_op jit(solution)/shard_map/cond/branch_1_fun/ppermute | solution.py:20
  77.3 1.4 %fusion.14 = (s32[1,1]{1,0:T(1,128)}, s32[1,1]{1,0:T(1,128)}) fusion(s32[32,32]{1,0:T(8,128)} %param.25, s32[]{:T(128)S(6)} %select_n.10, s32[]{:T(128)S(6)} %select_n.11, s32[]{:T(128)S(6)} %select_n.12), kind=kLoop, calls=%fused_computation.24 | loop fusion | bytes 28 | tf_op jit(solution)/shard_map/dynamic_slice | solution.py:70
  93.0 5.0 %fusion.8 = bf16[64,15,512]{2,0,1:T(8,128)(2,1)S(1)} fusion(bf16[15,64,2048]{2,1,0:T(8,128)(2,1)} %bitcast_dynamic-update-slice_fusion, bf16[512,2048]{1,0:T(8,128)(2,1)} %all-gather.3.cloned.1.call-done, f32[]{:T(128)} %bitcast.20), kind=kOutput, calls=%fused_computation.7 | convolution fusion | flops 2014248960 | bytes 7012356 | tf_op jit(solution)/shard_map/dot_general | solution.py:78
  99.5 21.6 %all-gather.5.cloned.1.call-done = bf16[512,2048]{1,0:T(8,128)(2,1)} async-done(((bf16[512,256]{1,0:T(8,128)(2,1)}), bf16[512,2048]{1,0:T(8,128)(2,1)}) %all-gather.5.cloned.1.call-update) | async-done | bytes 2097168 | tf_op jit(solution)/shard_map/all_gather | solution.py:77
  121.0 5.0 %fusion.11 = bf16[64,15,512]{2,0,1:T(8,128)(2,1)S(1)} fusion(bf16[15,64,2048]{2,1,0:T(8,128)(2,1)} %bitcast_dynamic-update-slice_fusion, bf16[512,2048]{1,0:T(8,128)(2,1)} %all-gather.5.cloned.1.call-done, f32[]{:T(128)} %bitcast.24), kind=kOutput, calls=%fused_computation.8 | convolution fusion | flops 2014248960 | bytes 7012356 | tf_op jit(solution)/shard_map/dot_general | solution.py:78
  127.6 3.3 %copy.18 = bf16[64,2,7680]{2,1,0:T(2,128)(2,1)} copy(bf16[64,2,7680]{2,0,1:T(8,128)(2,1)S(1)} %pad_maximum_fusion) | data formatting | bytes 3932160 | tf_op jit(solution)/shard_map/stack | solution.py:83
  (42 shorter events, 21.7 us)
Async XLA Ops:
  6.5 32.5 %copy-start = (bf16[512,256]{1,0:T(8,128)(2,1)S(1)}, bf16[512,256]{1,0:T(8,128)(2,1)}, u32[]{:S(2)}) copy-start(bf16[512,256]{1,0:T(8,128)(2,1)} %param.23) | copy-start | bytes 786436
  6.5 86.5 %all-gather.3.cloned.1.call-start = ((), (), s32[]{:S(2)}) async-start(), calls=%async_computation.2 | async-start | bytes 2359296 | tf_op jit(solution)/shard_map/all_gather | solution.py:77
  12.7 8.9 %collective-permute-start.1 = (bf16[512,256]{1,0:T(8,128)(2,1)}, bf16[512,256]{1,0:T(8,128)(2,1)S(1)}, u32[]{:S(2)}, u32[]{:S(2)}) collective-permute-start(bf16[512,256]{1,0:T(8,128)(2,1)} %param.3), channel_id=1, source_target_pairs={{0,16},{16,0},{8,24},{24,8},{32,48},{48,32},{40,56},{56,40},{64,80... | collective-permute-start | bytes 786440 | tf_op jit(solution)/shard_map/cond/branch_1_fun/ppermute | solution.py:20
  30.0 50.0 %all-to-all-start.1 = ((bf16[4,2,64,256]{3,2,1,0:T(8,128)(2,1)}), bf16[4,2,64,256]{3,2,1,0:T(8,128)(2,1)S(1)}, u32[]{:S(2)}, u32[]{:S(2)}) async-start(bf16[4,2,64,256]{3,2,1,0:T(8,128)(2,1)} %copy.13), calls=%async_computation.1 | async-start | bytes 524288 | tf_op jit(solution)/shard_map/all_to_all | solution.py:39
  35.6 85.5 %all-gather.5.cloned.1.call-start = ((), (), s32[]{:S(2)}) async-start(), calls=%async_computation.3 | async-start | bytes 2359296 | tf_op jit(solution)/shard_map/all_gather | solution.py:77
  39.0 7.4 %collective-permute-start.5 = (bf16[512,256]{1,0:T(8,128)(2,1)S(1)}, bf16[512,256]{1,0:T(8,128)(2,1)}, u32[]{:S(2)}, u32[]{:S(2)}) collective-permute-start(bf16[512,256]{1,0:T(8,128)(2,1)S(1)} %param.11), channel_id=1, source_target_pairs={{0,8},{8,0},{16,24},{24,16},{32,40},{40,32},{48,56},{56,48},{64,72... | collective-permute-start | bytes 786440 | tf_op jit(solution)/shard_map/cond/branch_1_fun/ppermute | solution.py:20
  46.5 6.5 %collective-permute-start.7 = (bf16[512,256]{1,0:T(8,128)(2,1)}, bf16[512,256]{1,0:T(8,128)(2,1)S(1)}, u32[]{:S(2)}, u32[]{:S(2)}) collective-permute-start(bf16[512,256]{1,0:T(8,128)(2,1)} %param.15), channel_id=1, source_target_pairs={{0,32},{32,0},{8,40},{40,8},{16,48},{48,16},{24,56},{56,24},{64,96... | collective-permute-start | bytes 786440 | tf_op jit(solution)/shard_map/cond/branch_1_fun/ppermute | solution.py:20
  53.7 7.2 %collective-permute-start.8 = (bf16[512,256]{1,0:T(8,128)(2,1)}, bf16[512,256]{1,0:T(8,128)(2,1)S(1)}, u32[]{:S(2)}, u32[]{:S(2)}) collective-permute-start(bf16[512,256]{1,0:T(8,128)(2,1)} %param.17), channel_id=1, source_target_pairs={{0,64},{64,0},{8,72},{72,8},{16,80},{80,16},{24,88},{88,24},{32,96... | collective-permute-start | bytes 786440 | tf_op jit(solution)/shard_map/cond/branch_1_fun/ppermute | solution.py:20
  61.6 13.7 %collective-permute-start.9 = (bf16[512,256]{1,0:T(8,128)(2,1)}, bf16[512,256]{1,0:T(8,128)(2,1)S(1)}, u32[]{:S(2)}, u32[]{:S(2)}) collective-permute-start(bf16[512,256]{1,0:T(8,128)(2,1)} %param.19), channel_id=1, source_target_pairs={{0,128},{128,0},{8,136},{136,8},{16,144},{144,16},{24,152},{152,24... | collective-permute-start | bytes 786440 | tf_op jit(solution)/shard_map/cond/branch_1_fun/ppermute | solution.py:20
Sparse Core Ops, SparseCore 0:
  22.4 46.4 all-gather.2
  76.1 44.8 all-gather.4
where the time goes:
time: 138 us
  waiting for transfers between devices  50.6 us (37%)
  local copies, waits for them, and re-layouts  28 us (20%)
  between operations  22.6 us (16%)
  starting transfers between devices  20.2 us (15%)
  matrix products  10.1 us (7%)
  blocking collectives  6.05 us (4%)
    ppermute x5, waiting for transfers between devices, swapped(): return lax.ppermute(block, axis, route)  28.9 us
    all_gather x2, waiting for transfers between devices, on_device(): gathered = lax.all_gather(current, TM, axis=1, tiled=True)  21.6 us
    ppermute x5, starting transfers between devices, swapped(): return lax.ppermute(block, axis, route)  14.7 us
    unnamed x16, local copies, waits for them, and re-layouts  11.8 us
    dot_general x2, matrix products, on_device(): lax.dot_general(own_shifted, gathered, (((2,), (1,)), ((), ())), preferre...  10.1 us
    all_to_all x1, blocking collectives, exchange_in_order(): lax.all_to_all(blocks, axes[k], split_axis=k, concat_axis=k, tiled=True)  6.05 us
    all_to_all x1, starting transfers between devices, exchange_in_order(): lax.all_to_all(blocks, axes[k], split_axis=k, concat_axis=k, tiled=True)  5.55 us
    cond x5, local copies, waits for them, and re-layouts  4.57 us
  transfers between devices with their start and end apart: 8, of which 6 were waited for; matrix products, arithmetic and copies ran while one was open for 18% of the time, Pallas kernels for 0%

commit v1 on v0

v1 whole, which is shorter than its diff:
```python
import functools

import jax
import jax.numpy as jnp
from jax import lax
from jax.experimental import pallas as pl
from jax.experimental.pallas import tpu as pltpu
from jax.sharding import Mesh
from jax.sharding import PartitionSpec as P

LAG = 7
LAGS = 2 * LAG + 1
TM = ("tm_0", "tm_1")
BLK_TM = ("blk", "tm_0", "tm_1")
GROUP = 3
VMEM_BYTES = 20 * 1024 * 1024

def swapped(value, axis, word):
    count = lax.axis_size(axis)
    return lax.ppermute(value, axis, [(i, i ^ word) for i in range(count)])


def crossed(value, word):
    count = lax.axis_size("blk") * 4
    return lax.ppermute(value, ("blk", "tm_0"), [(i, i ^ 64 ^ word) for i in range(count)])


def together(*values):
    return lax.optimization_barrier(values)


def by_word(value, word, count, move):
    return lax.switch(word, [functools.partial(move, word=k) for k in range(count)], value)


def to_near(value, word):
    return swapped(value, "blk", word) if word else value


def vmem():
    return pl.BlockSpec(memory_space=pltpu.VMEM)


def smem():
    return pl.BlockSpec(memory_space=pltpu.SMEM)


def params():
    return pltpu.CompilerParams(vmem_limit_bytes=VMEM_BYTES)


def cost(flops, size):
    return pl.CostEstimate(flops=flops, bytes_accessed=size, transcendentals=0)


def own_kernel(place_ref, here_ref, there_ref, out_ref, row_ref):
    z, core = place_ref[0], place_ref[1]
    rows, edge = row_ref.shape[0], 128
    row_ref[:, :edge] = jnp.zeros((rows, edge), row_ref.dtype)
    row_ref[:, edge + 2048 :] = jnp.zeros((rows, edge), row_ref.dtype)
    mine = pl.ds(pl.multiple_of(512 + core * rows, 64), rows)
    for k in range(4):
        slab = 2 * (z ^ k)
        for pack, at in ((here_ref, slab + core), (there_ref, slab + 1 - core)):
            row_ref[:, pl.ds(pl.multiple_of(edge + at * 256, 128), 256)] = pack[k, mine, :]
    for lag in range(LAGS):
        start = edge + LAG - lag
        out_ref[lag * rows : lag * rows + rows, :] = row_ref[:, start : start + 2048]


def own_shifts(place, here, there):
    return pl.pallas_call(
        own_kernel,
        in_specs=[smem()] + [vmem()] * 2,
        out_specs=vmem(),
        out_shape=jax.ShapeDtypeStruct((LAGS * 64, 2048), jnp.bfloat16),
        scratch_shapes=[pltpu.VMEM((64, 2048 + 256), jnp.bfloat16)],
        compiler_params=params(),
        cost_estimate=cost(0, 8_000_000),
    )(place, here, there)


def products(order_ref, own_ref, slab_refs):
    total = None
    for k, slab in enumerate(slab_refs):
        start = pl.multiple_of(order_ref[k] * 256, 256)
        part = lax.dot_general(
            own_ref[:, pl.ds(start, 256)], slab[:512, :], (((1,), (1,)), ((), ())), preferred_element_type=jnp.float32
        )
        total = part if total is None else total + part
    return total


def sums_kernel(count, order_ref, own_ref, *refs):
    total = products(order_ref, own_ref, refs[:count])
    refs[-1][...] = total + refs[count][...] if len(refs) > count + 1 else total


def sums(order, own, slabs, before=()):
    count = len(slabs)
    return pl.pallas_call(
        functools.partial(sums_kernel, count),
        in_specs=[smem(), vmem()] + [vmem()] * (count + len(before)),
        out_specs=vmem(),
        out_shape=jax.ShapeDtypeStruct((LAGS * 64, 512), jnp.float32),
        compiler_params=params(),
        cost_estimate=cost(2 * 960 * 512 * 256 * count, 2_000_000),
    )(order, own, *slabs, *before)


def place_round(out_ref, index, values, lags):
    for k in range(lags):
        rows = values[k * 64 : k * 64 + 64].astype(out_ref.dtype)
        out_ref[:, index, k * 512 : k * 512 + 512] = rows


def near_kernel(order_ref, weight_ref, own_ref, here_ref, there_ref, out_ref, sum_ref):
    slabs = [ref.at[k] for ref in (here_ref, there_ref) for k in range(4)]
    sum_ref[...] = products(order_ref, own_ref, slabs) * weight_ref[0]
    for index in range(2):
        @pl.when(order_ref[8] == index)
        def _():
            place_round(out_ref, index, sum_ref, LAGS)


def near_round(order, weights, own, here, there):
    return pl.pallas_call(
        near_kernel,
        in_specs=[smem(), smem()] + [vmem()] * 3,
        out_specs=vmem(),
        out_shape=jax.ShapeDtypeStruct((64, 2, LAGS * 512), jnp.bfloat16),
        scratch_shapes=[pltpu.VMEM((LAGS * 64, 512), jnp.float32)],
        compiler_params=params(),
        cost_estimate=cost(2 * 960 * 512 * 256 * 8, 4_000_000),
    )(order, weights, own, here, there)


def last_kernel(count, order_ref, weight_ref, own_ref, near_ref, part_ref, *refs):
    out_ref, sum_ref = refs[count], refs[count + 1]
    step = pl.program_id(0)

    @pl.when(step == 0)
    def _():
        sum_ref[...] = (products(order_ref, own_ref, refs[:count]) + part_ref[...]) * weight_ref[1]

    width = GROUP * 512
    out_ref[...] = near_ref[:, :, pl.ds(pl.multiple_of(step * width, width), width)]
    rows = sum_ref.at[pl.ds(pl.multiple_of(step * GROUP * 64, GROUP * 64), GROUP * 64)]
    for index in range(2):
        @pl.when(order_ref[count] != index)
        def _():
            place_round(out_ref, index, rows, GROUP)


def last_round(order, weights, own, near, part, slabs):
    count = len(slabs)
    return pl.pallas_call(
        functools.partial(last_kernel, count),
        grid=(LAGS // GROUP,),
        in_specs=[smem(), smem()] + [vmem()] * (3 + count),
        out_specs=pl.BlockSpec((64, 2, GROUP * 512), lambda g: (0, 0, g)),
        out_shape=jax.ShapeDtypeStruct((64, 2, LAGS * 512), jnp.bfloat16),
        scratch_shapes=[pltpu.VMEM((LAGS * 64, 512), jnp.float32)],
        compiler_params=params(),
        cost_estimate=cost(2 * 960 * 512 * 256 * count, 6_000_000),
    )(order, weights, own, near, part, *slabs)


def on_device(returns, plan, pair_mask):
    block = lax.axis_index("blk")
    z = lax.axis_index("tm_0")
    core = lax.axis_index("tm_1")
    minutes_all = returns.shape[1] * 8
    factor = float(minutes_all) ** (-0.5)

    words = (plan[0, 0], plan[1, 0])
    swap = (words[1] & 16) == 0
    near_word = jnp.where(swap, words[1], words[0])
    far_word = jnp.where(swap, words[0], words[1])
    near_live = pair_mask[block, block ^ near_word].astype(jnp.float32)
    far_live = pair_mask[block, block ^ far_word].astype(jnp.float32)
    weights = jnp.stack([near_live, far_live]) * factor

    def other_core(slabs):
        return [swapped(s, "tm_1", 1) for s in slabs]

    def order_of(words, extra=()):
        here = [2 * (z ^ k) + core for k in words]
        there = [2 * (z ^ k) + (1 - core) for k in words]
        return jnp.stack([jnp.int32(v) for v in here + there + list(extra)])

    near = by_word(returns, near_word & 15, 16, to_near)
    near = lax.cond(near_word >= 16, lambda v: swapped(v, "blk", 16), lambda v: v, near)
    rows = returns.reshape(4, 128, returns.shape[1])
    packs = []
    for k in range(4):
        pack = jnp.concatenate([near, lax.dynamic_index_in_dim(rows, z ^ k, 0, keepdims=False)], axis=0)
        packs.append(swapped(pack, "tm_0", k) if k else pack)
    far_word, _ = together(far_word, near)
    far = by_word(returns, far_word & 15, 16, to_near)
    far_2, far_1 = crossed(far, 2), crossed(far, 1)
    far_3, far_0 = swapped(far_2, "tm_0", 1), swapped(far_1, "tm_0", 1)
    packs = list(together(*packs, far_2, far_1)[:4])
    near_here = jnp.stack(packs)
    near_there = swapped(near_here, "tm_1", 1)
    own = own_shifts(jnp.stack([z, core]).astype(jnp.int32), near_here, near_there)
    near_index = swap.astype(jnp.int32)
    done = near_round(order_of(range(4), [near_index]), weights, own, near_here, near_there)
    part = sums(order_of([2, 1]), own, [far_2, far_1] + other_core([far_2, far_1]))
    far_3, far_0, done, part = together(far_3, far_0, done, part)
    order = order_of([3, 0])
    part = sums(order[:2], own, [far_3, far_0], (part,))
    order = jnp.concatenate([order[2:], near_index.reshape(1)])
    return last_round(order, weights, own, done, part, other_core([far_3, far_0]))


def solution(mesh):
    split = Mesh(mesh.devices.reshape(mesh.shape["blk"], 4, 2), ("blk", "tm_0", "tm_1"))
    return jax.shard_map(
        on_device,
        mesh=split,
        in_specs=(P("blk", TM), P(), P()),
        out_specs=P(BLK_TM, None, None),
        check_vma=False,
    )
```

time: 138 us -> 89.4 us (0.65)
  local copies, waits for them, and re-layouts: 28 us -> 3.78 us
  between operations: 22.6 us -> 4.41 us
  Pallas kernels: 0 us -> 12.6 us
  matrix products: 10.1 us -> 0 us
  waiting for transfers between devices: 50.6 us -> 41.4 us
  blocking collectives: 6.05 us -> 0 us
  starting transfers between devices: 20.2 us -> 25.1 us
  other arithmetic: 0.18 us -> 1.58 us
    all_gather x2 -> x0, waiting for transfers between devices: 21.6 us -> none  [on_device(): gathered = lax.all_gather(current, TM, axis=1, tiled=True)]
    pallas_call x0 -> x5, Pallas kernels: none -> 12.6 us  [the longest x1 3.96 us: last_round(): pl.pallas_call(functools.partial(last_kernel, count), grid=(LAGS // GROUP...]
    ppermute x5 -> x14, waiting for transfers between devices: 28.9 us -> 41.4 us  [the longest x2 27.1 us: crossed(): lax.ppermute(value, ('blk', 'tm_0'), [(i, i ^ 64 ^ word) for i in range(c...]
    unnamed x16 -> x2, local copies, waits for them, and re-layouts: 11.8 us -> 0.01 us
    ppermute x5 -> x14, starting transfers between devices: 14.7 us -> 25.1 us  [the longest x12 19.9 us: swapped(): return lax.ppermute(value, axis, [(i, i ^ word) for i in range(count)])]
    dot_general x2 -> x0, matrix products: 10.1 us -> none  [on_device(): lax.dot_general(own_shifted, gathered, (((2,), (1,)), ((), ())), preferre...]
    all_to_all x1 -> x0, blocking collectives: 6.05 us -> none  [exchange_in_order(): lax.all_to_all(blocks, axes[k], split_axis=k, concat_axis=k, tiled=True)]
    all_to_all x1 -> x0, starting transfers between devices: 5.55 us -> none  [exchange_in_order(): lax.all_to_all(blocks, axes[k], split_axis=k, concat_axis=k, tiled=True)]
  transfers between devices with their start and end apart: 8 -> 14, of which waited for: 6 -> 6; matrix products, arithmetic and copies ran while one was open for 18% -> 2% of each run, Pallas kernels for 0% -> 10%
where the time goes in v1:
time: 89.4 us; the launch traced here: 89.1 us
  waiting for transfers between devices  41.4 us (46%)
  starting transfers between devices  25.1 us (28%)
  Pallas kernels  12.6 us (14%)
  between operations  4.41 us (5%)
  local copies, waits for them, and re-layouts  3.78 us (4%)
  other arithmetic  1.58 us (2%)
    ppermute x2, waiting for transfers between devices, crossed(): lax.ppermute(value, ('blk', 'tm_0'), [(i, i ^ 64 ^ word) for i in range(c...  27.1 us
    ppermute x12, starting transfers between devices, swapped(): return lax.ppermute(value, axis, [(i, i ^ word) for i in range(count)])  19.9 us
    ppermute x12, waiting for transfers between devices, swapped(): return lax.ppermute(value, axis, [(i, i ^ word) for i in range(count)])  14.3 us
    ppermute x2, starting transfers between devices, crossed(): lax.ppermute(value, ('blk', 'tm_0'), [(i, i ^ 64 ^ word) for i in range(c...  5.18 us
    pallas_call x1, Pallas kernels, last_round(): pl.pallas_call(functools.partial(last_kernel, count), grid=(LAGS // GROUP...  3.96 us
    pallas_call x1, Pallas kernels, near_round(): pl.pallas_call(near_kernel, in_specs=[smem(), smem()] + [vmem()] * 3, out...  3.52 us
    pallas_call x2, Pallas kernels, sums(): pl.pallas_call(functools.partial(sums_kernel, count), in_specs=[smem(), v...  3.43 us
  transfers between devices with their start and end apart: 14, of which 6 were waited for; matrix products, arithmetic and copies ran while one was open for 2% of the time, Pallas kernels for 10%

profile of v1, /device:TPU:1, one launch (start us, length us, event | category | flops | bytes accessed | tf_op | source)
XLA Modules:
  0.0 89.1 jit_solution(7588889334900639404)
XLA Ops:
  0.0 1.3 %fusion.1 = (s32[1,1]{1,0:T(1,128)}, s32[1,1]{1,0:T(1,128)}) fusion(s32[2,32]{1,0:T(2,128)} %param.38), kind=kLoop, calls=%fused_computation.15 | loop fusion | bytes 16 | tf_op jit(solution)/shard_map/slice | solution.py:176
  3.1 10.0 %conditional.3 = (bf16[512,256]{1,0:T(8,128)(2,1)}) conditional(s32[]{:T(128)} %clamp.6, bf16[512,256]{1,0:T(8,128)(2,1)} %param.37, bf16[512,256]{1,0:T(8,128)(2,1)} %param.37, bf16[512,256]{1,0:T(8,128)(2,1)} %param.37, bf16[512,256]{1,0:T(8,128)(2,1)} %param.37, bf16[512,256]{1,0:T(8,128)(2,1)} %param.37, ...), branch_computations={%region_0.1_spmd, %region_1.2_spmd, %region_2.3_spmd, %region_3.4_... | conditional | bytes 1048624 | solution.py:33
  3.1 4.7 %collective-permute-start.5 = (bf16[512,256]{1,0:T(8,128)(2,1)}, bf16[512,256]{1,0:T(8,128)(2,1)}, u32[]{:S(2)}, u32[]{:S(2)}) collective-permute-start(bf16[512,256]{1,0:T(8,128)(2,1)} %param.6), channel_id=1, source_target_pairs={{0,48},{8,56},{16,32},{24,40},{32,16},{40,24},{48,0},{56,8},{64,11... | collective-permute-start | bytes 786440 | tf_op jit(solution)/shard_map/cond/branch_6_fun/ppermute | solution.py:20
  7.8 5.3 %collective-permute-done.5 = bf16[512,256]{1,0:T(8,128)(2,1)} collective-permute-done((bf16[512,256]{1,0:T(8,128)(2,1)}, bf16[512,256]{1,0:T(8,128)(2,1)}, u32[]{:S(2)}, u32[]{:S(2)}) %collective-permute-start.5) | collective-permute-done | bytes 262176 | tf_op jit(solution)/shard_map/cond/branch_6_fun/ppermute | solution.py:20
  13.1 1.0 %dynamic-slice_bitcast_fusion = (bf16[128,256]{1,0:T(8,128)(2,1)S(1)}, bf16[128,256]{1,0:T(8,128)(2,1)S(1)}, bf16[128,256]{1,0:T(8,128)(2,1)S(1)}, bf16[128,256]{1,0:T(8,128)(2,1)S(1)}) fusion(bf16[4,128,256]{2,1,0:T(8,128)(2,1)} %bitcast.28, s32[]{:T(128)S(6)} %select_n.38, s32[]{:T(128)S(6)} %select_n.37, s32[]{:T(128)S(6)} %select_n.36, s32[]{:T(128)S(6)} %select_n.35), kind=kLoop, calls=%fused_computation.5 | loop fusion | bytes 524304 | tf_op jit(solution)/shard_map/jit(dynamic_index_in_dim)/squeeze | solution.py:197
  14.1 1.0 %pad_maximum_fusion.4 = (bf16[640,256]{1,0:T(8,128)(2,1)S(1)}, bf16[640,256]{1,0:T(8,128)(2,1)S(1)}, bf16[640,256]{1,0:T(8,128)(2,1)S(1)}, bf16[640,256]{1,0:T(8,128)(2,1)S(1)}) fusion(bf16[128,256]{1,0:T(8,128)(2,1)S(1)} %get-tuple-element.98, bf16[512,256]{1,0:T(8,128)(2,1)} %get-tuple-element.107, bf16[128,256]{1,0:T(8,128)(2,1)S(1)} %get-tuple-element.100, ...), kind=kLoop, calls=%fused_computation.4 | loop fusion | flops 2129920 | bytes 1835008 | tf_op jit(solution)/shard_map/concatenate | solution.py:197
  15.1 2.6 %collective-permute-start.31 = (bf16[640,256]{1,0:T(8,128)(2,1)S(1)}, bf16[640,256]{1,0:T(8,128)(2,1)S(1)}, u32[]{:S(2)}, u32[]{:S(2)}) collective-permute-start(bf16[640,256]{1,0:T(8,128)(2,1)S(1)} %get-tuple-element.95), channel_id=1, source_target_pairs={{0,2},{2,0},{4,6},{6,4},{1,3},{3,1},{5,7},{7,5},{8,10},{10,8},{12,... | collective-permute-start | bytes 983048 | tf_op jit(solution)/shard_map/ppermute | solution.py:20
  17.7 3.0 %collective-permute-start.32 = (bf16[640,256]{1,0:T(8,128)(2,1)S(1)}, bf16[640,256]{1,0:T(8,128)(2,1)S(1)}, u32[]{:S(2)}, u32[]{:S(2)}) collective-permute-start(bf16[640,256]{1,0:T(8,128)(2,1)S(1)} %get-tuple-element.96), channel_id=1, source_target_pairs={{0,4},{2,6},{4,0},{6,2},{1,5},{3,7},{5,1},{7,3},{8,12},{10,14},{12... | collective-permute-start | bytes 983048 | tf_op jit(solution)/shard_map/ppermute | solution.py:20
  21.9 8.5 %conditional.5 = (bf16[512,256]{1,0:T(8,128)(2,1)}) conditional(s32[]{:T(128)} %clamp.7, bf16[512,256]{1,0:T(8,128)(2,1)S(1)} %copy-done, bf16[512,256]{1,0:T(8,128)(2,1)S(1)} %copy-done, bf16[512,256]{1,0:T(8,128)(2,1)S(1)} %copy-done, bf16[512,256]{1,0:T(8,128)(2,1)S(1)} %copy-done, ...), branch_computations={%region_18.19_spmd, %region_19.20_spmd, %region_20.21_spmd, %regio... | conditional | bytes 1048624 | solution.py:33
  22.1 3.9 %collective-permute-start.24 = (bf16[512,256]{1,0:T(8,128)(2,1)S(1)}, bf16[512,256]{1,0:T(8,128)(2,1)}, u32[]{:S(2)}, u32[]{:S(2)}) collective-permute-start(bf16[512,256]{1,0:T(8,128)(2,1)S(1)} %param.27), channel_id=1, source_target_pairs={{0,72},{8,64},{16,88},{24,80},{32,104},{40,96},{48,120},{56,112},{... | collective-permute-start | bytes 786440 | tf_op jit(solution)/shard_map/cond/branch_9_fun/ppermute | solution.py:20
  26.1 4.4 %collective-permute-done.24 = bf16[512,256]{1,0:T(8,128)(2,1)} collective-permute-done((bf16[512,256]{1,0:T(8,128)(2,1)S(1)}, bf16[512,256]{1,0:T(8,128)(2,1)}, u32[]{:S(2)}, u32[]{:S(2)}) %collective-permute-start.24) | collective-permute-done | bytes 262176 | tf_op jit(solution)/shard_map/cond/branch_9_fun/ppermute | solution.py:20
  30.4 3.6 %collective-permute-start.34 = (bf16[512,256]{1,0:T(8,128)(2,1)}, bf16[512,256]{1,0:T(8,128)(2,1)S(1)}, u32[]{:S(2)}, u32[]{:S(2)}) collective-permute-start(bf16[512,256]{1,0:T(8,128)(2,1)} %get-tuple-element.108), channel_id=1, source_target_pairs={{0,132},{2,134},{4,128},{6,130},{8,140},{10,142},{12,136},{14,138}... | collective-permute-start | bytes 786440 | tf_op jit(solution)/shard_map/ppermute | solution.py:25
  34.0 1.6 %collective-permute-start.35 = (bf16[512,256]{1,0:T(8,128)(2,1)}, bf16[512,256]{1,0:T(8,128)(2,1)S(1)}, u32[]{:S(2)}, u32[]{:S(2)}) collective-permute-start(bf16[512,256]{1,0:T(8,128)(2,1)} %get-tuple-element.108), channel_id=1, source_target_pairs={{0,130},{2,128},{4,134},{6,132},{8,138},{10,136},{12,142},{14,140}... | collective-permute-start | bytes 786440 | tf_op jit(solution)/shard_map/ppermute | solution.py:25
  35.6 8.1 %collective-permute-done.34.refs_0_ = bf16[512,256]{1,0:T(8,128)(2,1)S(1)} collective-permute-done((bf16[512,256]{1,0:T(8,128)(2,1)}, bf16[512,256]{1,0:T(8,128)(2,1)S(1)}, u32[]{:S(2)}, u32[]{:S(2)}) %collective-permute-start.34) | collective-permute-done | bytes 262176 | tf_op jit(solution)/shard_map/ppermute | solution.py:25
  43.7 19.1 %collective-permute-done.35.refs_1_ = bf16[512,256]{1,0:T(8,128)(2,1)S(1)} collective-permute-done((bf16[512,256]{1,0:T(8,128)(2,1)}, bf16[512,256]{1,0:T(8,128)(2,1)S(1)}, u32[]{:S(2)}, u32[]{:S(2)}) %collective-permute-start.35) | collective-permute-done | bytes 262176 | tf_op jit(solution)/shard_map/ppermute | solution.py:25
  62.9 2.8 %collective-permute-start.36 = (bf16[4,640,256]{2,1,0:T(8,128)(2,1)S(1)}, bf16[4,640,256]{2,1,0:T(8,128)(2,1)S(1)}, u32[]{:S(2)}, u32[]{:S(2)}) collective-permute-start(bf16[4,640,256]{2,1,0:T(8,128)(2,1)S(1)} %pad_maximum_fusion.here_ref), channel_id=1, source_target_pairs={{0,1},{1,0},{2,3},{3,2},{4,5},{5,4},{6,7},{7,6},{8,9},{9,8},{10,11... | collective-permute-start | bytes 3932168 | tf_op jit(solution)/shard_map/ppermute | solution.py:20
  66.3 1.4 %fusion = (s32[1,1]{1,0:T(1,128)}, s32[1,1]{1,0:T(1,128)}) fusion(s32[32,32]{1,0:T(8,128)} %param.39, s32[]{:T(128)S(6)} %select_n.30, s32[]{:T(128)S(6)} %select_n.32, s32[]{:T(128)S(6)} %select_n.34), kind=kLoop, calls=%fused_computation.14 | loop fusion | bytes 28 | tf_op jit(solution)/shard_map/dynamic_slice | solution.py:180
  69.3 1.5 %collective-permute-start.38 = (bf16[512,256]{1,0:T(8,128)(2,1)S(1)}, bf16[512,256]{1,0:T(8,128)(2,1)S(1)}, u32[]{:S(2)}, u32[]{:S(2)}) collective-permute-start(bf16[512,256]{1,0:T(8,128)(2,1)S(1)} %collective-permute-done.35.refs_1_), channel_id=1, source_target_pairs={{0,2},{2,0},{4,6},{6,4},{1,3},{3,1},{5,7},{7,5},{8,10},{10,8},{12,... | collective-permute-start | bytes 786440 | tf_op jit(solution)/shard_map/ppermute | solution.py:20
  70.7 1.7 %shard_map.133.own_ref = bf16[960,2048]{1,0:T(8,128)(2,1)S(1)} custom-call(s32[2]{0:T(128)S(1)} %pad_add_fusion.1.place_ref, bf16[4,640,256]{2,1,0:T(8,128)(2,1)S(1)} %pad_maximum_fusion.here_ref, bf16[4,640,256]{2,1,0:T(8,128)(2,1)S(1)} %collective-permute-done.36.there_ref), custom_call_target="tpu_custom_call" | custom-call | bytes 8000000 | tf_op jit(solution)/shard_map/pallas_call | solution.py:72
  72.5 2.2 %shard_map.135.refs_2_ = f32[960,512]{1,0:T(8,128)S(1)} custom-call(s32[4]{0:T(128)S(1)} %pad_add_fusion.2.order_ref, bf16[960,2048]{1,0:T(8,128)(2,1)S(1)} %shard_map.133.own_ref, bf16[512,256]{1,0:T(8,128)(2,1)S(1)} %collective-permute-done.34.refs_0_, bf16[512,256]{1,0:T(8,128)(2,1)S(1)} %collective-permute-done.35.refs_1_, ...), custom_call_target="tpu_custom_call" | custom-call | flops 1006632960 | bytes 2000000 | tf_op jit(solution)/shard_map/pallas_call | solution.py:101
  74.6 3.5 %shard_map.134.near_ref = bf16[64,2,7680]{2,1,0:T(2,128)(2,1)S(1)} custom-call(s32[9]{0:T(128)S(1)} %stack.94.order_ref, f32[2]{0:T(128)S(1)} %maximum_multiply_fusion.weight_ref, bf16[960,2048]{1,0:T(8,128)(2,1)S(1)} %shard_map.133.own_ref, bf16[4,640,256]{2,1,0:T(8,128)(2,1)S(1)} %pad_maximum_fusion.here_ref, ...), custom_call_target="tpu_custom_call" | custom-call | flops 2013265920 | bytes 4000000 | tf_op jit(solution)/shard_map/pallas_call | solution.py:127
  78.2 4.5 %collective-permute-done.38.refs_1_ = bf16[512,256]{1,0:T(8,128)(2,1)S(1)} collective-permute-done((bf16[512,256]{1,0:T(8,128)(2,1)S(1)}, bf16[512,256]{1,0:T(8,128)(2,1)S(1)}, u32[]{:S(2)}, u32[]{:S(2)}) %collective-permute-start.38) | collective-permute-done | bytes 262176 | tf_op jit(solution)/shard_map/ppermute | solution.py:20
  83.8 1.3 %shard_map.136.part_ref = f32[960,512]{1,0:T(8,128)S(1)} custom-call(s32[2]{0:T(128)S(1)} %pad_add_fusion.3.order_ref, bf16[960,2048]{1,0:T(8,128)(2,1)S(1)} %shard_map.133.own_ref, bf16[512,256]{1,0:T(8,128)(2,1)S(1)} %collective-permute-done.37.refs_0_, bf16[512,256]{1,0:T(8,128)(2,1)S(1)} %collective-permute-done.38.refs_1_, ...), custom_call_target="tpu_custom_call" | custom-call | flops 503316480 | bytes 2000000 | tf_op jit(solution)/shard_map/pallas_call | solution.py:101
  85.2 4.0 %shard_map.137 = bf16[64,2,7680]{2,1,0:T(2,128)(2,1)} custom-call(s32[3]{0:T(128)S(1)} %pad_add_fusion.order_ref, f32[2]{0:T(128)S(1)} %maximum_multiply_fusion.weight_ref, bf16[960,2048]{1,0:T(8,128)(2,1)S(1)} %shard_map.133.own_ref, bf16[64,2,7680]{2,1,0:T(2,128)(2,1)S(1)} %shard_map.134.near_ref, f32[960,512]{1,0:T(8,128)S(1)} %shard_map.136.part_ref, ...), custom_call_target="tpu_custom_call" | custom-call | flops 503316480 | bytes 6000000 | tf_op jit(solution)/shard_map/pallas_call | solution.py:157
  (25 shorter events, 2.3 us)
Async XLA Ops:
  3.1 10.0 %collective-permute-start.5 = (bf16[512,256]{1,0:T(8,128)(2,1)}, bf16[512,256]{1,0:T(8,128)(2,1)}, u32[]{:S(2)}, u32[]{:S(2)}) collective-permute-start(bf16[512,256]{1,0:T(8,128)(2,1)} %param.6), channel_id=1, source_target_pairs={{0,48},{8,56},{16,32},{24,40},{32,16},{40,24},{48,0},{56,8},{64,11... | collective-permute-start | bytes 786440 | tf_op jit(solution)/shard_map/cond/branch_6_fun/ppermute | solution.py:20
  13.1 8.8 %copy-start = (bf16[512,256]{1,0:T(8,128)(2,1)S(1)}, bf16[512,256]{1,0:T(8,128)(2,1)}, u32[]{:S(2)}) copy-start(bf16[512,256]{1,0:T(8,128)(2,1)} %param.37) | copy-start | bytes 786436
  15.1 47.6 %collective-permute-start.31 = (bf16[640,256]{1,0:T(8,128)(2,1)S(1)}, bf16[640,256]{1,0:T(8,128)(2,1)S(1)}, u32[]{:S(2)}, u32[]{:S(2)}) collective-permute-start(bf16[640,256]{1,0:T(8,128)(2,1)S(1)} %get-tuple-element.95), channel_id=1, source_target_pairs={{0,2},{2,0},{4,6},{6,4},{1,3},{3,1},{5,7},{7,5},{8,10},{10,8},{12,... | collective-permute-start | bytes 983048 | tf_op jit(solution)/shard_map/ppermute | solution.py:20
  17.7 45.1 %collective-permute-start.32 = (bf16[640,256]{1,0:T(8,128)(2,1)S(1)}, bf16[640,256]{1,0:T(8,128)(2,1)S(1)}, u32[]{:S(2)}, u32[]{:S(2)}) collective-permute-start(bf16[640,256]{1,0:T(8,128)(2,1)S(1)} %get-tuple-element.96), channel_id=1, source_target_pairs={{0,4},{2,6},{4,0},{6,2},{1,5},{3,7},{5,1},{7,3},{8,12},{10,14},{12... | collective-permute-start | bytes 983048 | tf_op jit(solution)/shard_map/ppermute | solution.py:20
  20.7 42.1 %collective-permute-start.33 = (bf16[640,256]{1,0:T(8,128)(2,1)S(1)}, bf16[640,256]{1,0:T(8,128)(2,1)S(1)}, u32[]{:S(2)}, u32[]{:S(2)}) collective-permute-start(bf16[640,256]{1,0:T(8,128)(2,1)S(1)} %get-tuple-element.94), channel_id=1, source_target_pairs={{0,6},{2,4},{4,2},{6,0},{1,7},{3,5},{5,3},{7,1},{8,14},{10,12},{12... | collective-permute-start | bytes 983048 | tf_op jit(solution)/shard_map/ppermute | solution.py:20
  22.1 8.3 %collective-permute-start.24 = (bf16[512,256]{1,0:T(8,128)(2,1)S(1)}, bf16[512,256]{1,0:T(8,128)(2,1)}, u32[]{:S(2)}, u32[]{:S(2)}) collective-permute-start(bf16[512,256]{1,0:T(8,128)(2,1)S(1)} %param.27), channel_id=1, source_target_pairs={{0,72},{8,64},{16,88},{24,80},{32,104},{40,96},{48,120},{56,112},{... | collective-permute-start | bytes 786440 | tf_op jit(solution)/shard_map/cond/branch_9_fun/ppermute | solution.py:20
  30.4 13.2 %collective-permute-start.34 = (bf16[512,256]{1,0:T(8,128)(2,1)}, bf16[512,256]{1,0:T(8,128)(2,1)S(1)}, u32[]{:S(2)}, u32[]{:S(2)}) collective-permute-start(bf16[512,256]{1,0:T(8,128)(2,1)} %get-tuple-element.108), channel_id=1, source_target_pairs={{0,132},{2,134},{4,128},{6,130},{8,140},{10,142},{12,136},{14,138}... | collective-permute-start | bytes 786440 | tf_op jit(solution)/shard_map/ppermute | solution.py:25
  34.0 28.7 %collective-permute-start.35 = (bf16[512,256]{1,0:T(8,128)(2,1)}, bf16[512,256]{1,0:T(8,128)(2,1)S(1)}, u32[]{:S(2)}, u32[]{:S(2)}) collective-permute-start(bf16[512,256]{1,0:T(8,128)(2,1)} %get-tuple-element.108), channel_id=1, source_target_pairs={{0,130},{2,128},{4,134},{6,132},{8,138},{10,136},{12,142},{14,140}... | collective-permute-start | bytes 786440 | tf_op jit(solution)/shard_map/ppermute | solution.py:25
  62.9 7.8 %collective-permute-start.36 = (bf16[4,640,256]{2,1,0:T(8,128)(2,1)S(1)}, bf16[4,640,256]{2,1,0:T(8,128)(2,1)S(1)}, u32[]{:S(2)}, u32[]{:S(2)}) collective-permute-start(bf16[4,640,256]{2,1,0:T(8,128)(2,1)S(1)} %pad_maximum_fusion.here_ref), channel_id=1, source_target_pairs={{0,1},{1,0},{2,3},{3,2},{4,5},{5,4},{6,7},{7,6},{8,9},{9,8},{10,11... | collective-permute-start | bytes 3932168 | tf_op jit(solution)/shard_map/ppermute | solution.py:20
  65.7 6.7 %collective-permute-start.39 = (bf16[512,256]{1,0:T(8,128)(2,1)S(1)}, bf16[512,256]{1,0:T(8,128)(2,1)S(1)}, u32[]{:S(2)}, u32[]{:S(2)}) collective-permute-start(bf16[512,256]{1,0:T(8,128)(2,1)S(1)} %collective-permute-done.34.refs_0_), channel_id=1, source_target_pairs={{0,1},{1,0},{2,3},{3,2},{4,5},{5,4},{6,7},{7,6},{8,9},{9,8},{10,11... | collective-permute-start | bytes 786440 | tf_op jit(solution)/shard_map/ppermute | solution.py:20
  65.8 6.6 %collective-permute-start.40 = (bf16[512,256]{1,0:T(8,128)(2,1)S(1)}, bf16[512,256]{1,0:T(8,128)(2,1)}, u32[]{:S(2)}, u32[]{:S(2)}) collective-permute-start(bf16[512,256]{1,0:T(8,128)(2,1)S(1)} %collective-permute-done.35.refs_1_), channel_id=1, source_target_pairs={{0,1},{1,0},{2,3},{3,2},{4,5},{5,4},{6,7},{7,6},{8,9},{9,8},{10,11... | collective-permute-start | bytes 786440 | tf_op jit(solution)/shard_map/ppermute | solution.py:20
  69.3 8.9 %collective-permute-start.37 = (bf16[512,256]{1,0:T(8,128)(2,1)S(1)}, bf16[512,256]{1,0:T(8,128)(2,1)S(1)}, u32[]{:S(2)}, u32[]{:S(2)}) collective-permute-start(bf16[512,256]{1,0:T(8,128)(2,1)S(1)} %collective-permute-done.34.refs_0_), channel_id=1, source_target_pairs={{0,2},{2,0},{4,6},{6,4},{1,3},{3,1},{5,7},{7,5},{8,10},{10,8},{12,... | collective-permute-start | bytes 786440 | tf_op jit(solution)/shard_map/ppermute | solution.py:20
  69.3 13.4 %collective-permute-start.38 = (bf16[512,256]{1,0:T(8,128)(2,1)S(1)}, bf16[512,256]{1,0:T(8,128)(2,1)S(1)}, u32[]{:S(2)}, u32[]{:S(2)}) collective-permute-start(bf16[512,256]{1,0:T(8,128)(2,1)S(1)} %collective-permute-done.35.refs_1_), channel_id=1, source_target_pairs={{0,2},{2,0},{4,6},{6,4},{1,3},{3,1},{5,7},{7,5},{8,10},{10,8},{12,... | collective-permute-start | bytes 786440 | tf_op jit(solution)/shard_map/ppermute | solution.py:20
  82.7 2.4 %collective-permute-start.41 = (bf16[512,256]{1,0:T(8,128)(2,1)S(1)}, bf16[512,256]{1,0:T(8,128)(2,1)S(1)}, u32[]{:S(2)}, u32[]{:S(2)}) collective-permute-start(bf16[512,256]{1,0:T(8,128)(2,1)S(1)} %collective-permute-done.37.refs_0_), channel_id=1, source_target_pairs={{0,1},{1,0},{2,3},{3,2},{4,5},{5,4},{6,7},{7,6},{8,9},{9,8},{10,11... | collective-permute-start | bytes 786440 | tf_op jit(solution)/shard_map/ppermute | solution.py:20
  83.6 1.5 %collective-permute-start.42 = (bf16[512,256]{1,0:T(8,128)(2,1)S(1)}, bf16[512,256]{1,0:T(8,128)(2,1)S(1)}, u32[]{:S(2)}, u32[]{:S(2)}) collective-permute-start(bf16[512,256]{1,0:T(8,128)(2,1)S(1)} %collective-permute-done.38.refs_1_), channel_id=1, source_target_pairs={{0,1},{1,0},{2,3},{3,2},{4,5},{5,4},{6,7},{7,6},{8,9},{9,8},{10,11... | collective-permute-start | bytes 786440 | tf_op jit(solution)/shard_map/ppermute | solution.py:20

commit v2 on v1

--- a/solution.py
+++ b/solution.py
@@ -12,7 +12,7 @@
 LAGS = 2 * LAG + 1
 TM = ("tm_0", "tm_1")
 BLK_TM = ("blk", "tm_0", "tm_1")
-GROUP = 3
+GROUP = 5
 VMEM_BYTES = 20 * 1024 * 1024
 
 def swapped(value, axis, word):
@@ -189,6 +189,9 @@
         there = [2 * (z ^ k) + (1 - core) for k in words]
         return jnp.stack([jnp.int32(v) for v in here + there + list(extra)])
 
+    far = by_word(returns, far_word & 15, 16, to_near)
+    far_2, far_1 = crossed(far, 2), crossed(far, 1)
+    near_word, _ = together(near_word, far)
     near = by_word(returns, near_word & 15, 16, to_near)
     near = lax.cond(near_word >= 16, lambda v: swapped(v, "blk", 16), lambda v: v, near)
     rows = returns.reshape(4, 128, returns.shape[1])
@@ -196,11 +199,9 @@
     for k in range(4):
         pack = jnp.concatenate([near, lax.dynamic_index_in_dim(rows, z ^ k, 0, keepdims=False)], axis=0)
         packs.append(swapped(pack, "tm_0", k) if k else pack)
-    far_word, _ = together(far_word, near)
-    far = by_word(returns, far_word & 15, 16, to_near)
-    far_2, far_1 = crossed(far, 2), crossed(far, 1)
+    far_2, far_1, weights = together(far_2, far_1, weights)
     far_3, far_0 = swapped(far_2, "tm_0", 1), swapped(far_1, "tm_0", 1)
-    packs = list(together(*packs, far_2, far_1)[:4])
+    packs = list(together(*packs, far_3, far_1)[:4])
     near_here = jnp.stack(packs)
     near_there = swapped(near_here, "tm_1", 1)
     own = own_shifts(jnp.stack([z, core]).astype(jnp.int32), near_here, near_there)

time: 89.4 us -> 87.4 us (0.978)
    ppermute x2, waiting for transfers between devices: 27.1 us -> 6.18 us  [crossed(): lax.ppermute(value, ('blk', 'tm_0'), [(i, i ^ 64 ^ word) for i in range(c...]
    ppermute x12, waiting for transfers between devices: 14.3 us -> 34.5 us  [swapped(): return lax.ppermute(value, axis, [(i, i ^ word) for i in range(count)])]
    ppermute x12, starting transfers between devices: 19.9 us -> 17 us  [swapped(): return lax.ppermute(value, axis, [(i, i ^ word) for i in range(count)])]
    ppermute x2, starting transfers between devices: 5.18 us -> 7.52 us  [crossed(): lax.ppermute(value, ('blk', 'tm_0'), [(i, i ^ 64 ^ word) for i in range(c...]
  transfers between devices with their start and end apart: 14 -> 14, of which waited for: 6 -> 9; matrix products, arithmetic and copies ran while one was open for 2% -> 4% of each run, Pallas kernels for 10% -> 10%
where the time goes in v2:
time: 87.4 us; the launch traced here: 87.1 us
  waiting for transfers between devices  40.7 us (47%)
  starting transfers between devices  24.5 us (28%)
  Pallas kernels  11.9 us (14%)
  between operations  4.59 us (5%)
  local copies, waits for them, and re-layouts  3.74 us (4%)
  other arithmetic  1.58 us (2%)
    ppermute x12, waiting for transfers between devices, swapped(): return lax.ppermute(value, axis, [(i, i ^ word) for i in range(count)])  34.5 us
    ppermute x12, starting transfers between devices, swapped(): return lax.ppermute(value, axis, [(i, i ^ word) for i in range(count)])  17 us
    ppermute x2, starting transfers between devices, crossed(): lax.ppermute(value, ('blk', 'tm_0'), [(i, i ^ 64 ^ word) for i in range(c...  7.52 us
    ppermute x2, waiting for transfers between devices, crossed(): lax.ppermute(value, ('blk', 'tm_0'), [(i, i ^ 64 ^ word) for i in range(c...  6.18 us
    pallas_call x2, Pallas kernels, sums(): pl.pallas_call(functools.partial(sums_kernel, count), in_specs=[smem(), v...  3.51 us
    pallas_call x1, Pallas kernels, last_round(): pl.pallas_call(functools.partial(last_kernel, count), grid=(LAGS // GROUP...  3.42 us
    pallas_call x1, Pallas kernels, near_round(): pl.pallas_call(near_kernel, in_specs=[smem(), smem()] + [vmem()] * 3, out...  3.27 us
  transfers between devices with their start and end apart: 14, of which 9 were waited for; matrix products, arithmetic and copies ran while one was open for 4% of the time, Pallas kernels for 10%

profile of v2, /device:TPU:1, one launch (start us, length us, event | category | flops | bytes accessed | tf_op | source)
XLA Modules:
  0.0 87.1 jit_solution(5760441907338409395)
XLA Ops:
  0.0 1.3 %fusion.1 = (s32[1,1]{1,0:T(1,128)}, s32[1,1]{1,0:T(1,128)}) fusion(s32[2,32]{1,0:T(2,128)} %param.38), kind=kLoop, calls=%fused_computation.15 | loop fusion | bytes 16 | tf_op jit(solution)/shard_map/slice | solution.py:176
  3.2 11.4 %conditional.3 = (bf16[512,256]{1,0:T(8,128)(2,1)}) conditional(s32[]{:T(128)} %clamp.6, bf16[512,256]{1,0:T(8,128)(2,1)} %param.37, bf16[512,256]{1,0:T(8,128)(2,1)} %param.37, bf16[512,256]{1,0:T(8,128)(2,1)} %param.37, bf16[512,256]{1,0:T(8,128)(2,1)} %param.37, bf16[512,256]{1,0:T(8,128)(2,1)} %param.37, ...), branch_computations={%region_0.1_spmd, %region_1.2_spmd, %region_2.3_spmd, %region_3.4_... | conditional | bytes 1048624 | solution.py:33
  3.3 6.0 %collective-permute-start.10 = (bf16[512,256]{1,0:T(8,128)(2,1)}, bf16[512,256]{1,0:T(8,128)(2,1)}, u32[]{:S(2)}, u32[]{:S(2)}) collective-permute-start(bf16[512,256]{1,0:T(8,128)(2,1)} %param.11), channel_id=1, source_target_pairs={{0,88},{8,80},{16,72},{24,64},{32,120},{40,112},{48,104},{56,96},{... | collective-permute-start | bytes 786440 | tf_op jit(solution)/shard_map/cond/branch_11_fun/ppermute | solution.py:20
  9.3 5.3 %collective-permute-done.10 = bf16[512,256]{1,0:T(8,128)(2,1)} collective-permute-done((bf16[512,256]{1,0:T(8,128)(2,1)}, bf16[512,256]{1,0:T(8,128)(2,1)}, u32[]{:S(2)}, u32[]{:S(2)}) %collective-permute-start.10) | collective-permute-done | bytes 262176 | tf_op jit(solution)/shard_map/cond/branch_11_fun/ppermute | solution.py:20
  14.6 6.8 %collective-permute-start.31 = (bf16[512,256]{1,0:T(8,128)(2,1)}, bf16[512,256]{1,0:T(8,128)(2,1)S(1)}, u32[]{:S(2)}, u32[]{:S(2)}) collective-permute-start(bf16[512,256]{1,0:T(8,128)(2,1)} %get-tuple-element.112), channel_id=1, source_target_pairs={{0,132},{2,134},{4,128},{6,130},{8,140},{10,142},{12,136},{14,138}... | collective-permute-start | bytes 786440 | tf_op jit(solution)/shard_map/ppermute | solution.py:25
  24.4 6.2 %conditional.4 = (bf16[512,256]{1,0:T(8,128)(2,1)}) conditional(s32[]{:T(128)} %clamp.7, bf16[512,256]{1,0:T(8,128)(2,1)} %param.37, bf16[512,256]{1,0:T(8,128)(2,1)} %param.37, bf16[512,256]{1,0:T(8,128)(2,1)} %param.37, bf16[512,256]{1,0:T(8,128)(2,1)} %param.37, bf16[512,256]{1,0:T(8,128)(2,1)} %param.37, ...), branch_computations={%region_16.17_spmd, %region_17.18_spmd, %region_18.19_spmd, %regio... | conditional | bytes 1048624 | solution.py:33
  24.4 1.3 %collective-permute-start.18 = (bf16[512,256]{1,0:T(8,128)(2,1)}, bf16[512,256]{1,0:T(8,128)(2,1)}, u32[]{:S(2)}, u32[]{:S(2)}) collective-permute-start(bf16[512,256]{1,0:T(8,128)(2,1)} %param.20), channel_id=1, source_target_pairs={{0,32},{8,40},{16,48},{24,56},{32,0},{40,8},{48,16},{56,24},{64,96... | collective-permute-start | bytes 786440 | tf_op jit(solution)/shard_map/cond/branch_4_fun/ppermute | solution.py:20
  25.7 4.8 %collective-permute-done.18 = bf16[512,256]{1,0:T(8,128)(2,1)} collective-permute-done((bf16[512,256]{1,0:T(8,128)(2,1)}, bf16[512,256]{1,0:T(8,128)(2,1)}, u32[]{:S(2)}, u32[]{:S(2)}) %collective-permute-start.18) | collective-permute-done | bytes 262176 | tf_op jit(solution)/shard_map/cond/branch_4_fun/ppermute | solution.py:20
  30.5 1.0 %pad_maximum_fusion.4 = (bf16[640,256]{1,0:T(8,128)(2,1)S(1)}, bf16[640,256]{1,0:T(8,128)(2,1)S(1)}, bf16[640,256]{1,0:T(8,128)(2,1)S(1)}, bf16[640,256]{1,0:T(8,128)(2,1)S(1)}) fusion(bf16[128,256]{1,0:T(8,128)(2,1)S(1)} %get-tuple-element.104, bf16[512,256]{1,0:T(8,128)(2,1)} %get-tuple-element.114, bf16[128,256]{1,0:T(8,128)(2,1)S(1)} %get-tuple-element.106, ...), kind=kLoop, calls=%fused_computation.4 | loop fusion | flops 2129920 | bytes 1835008 | tf_op jit(solution)/shard_map/concatenate | solution.py:200
  32.4 1.2 %collective-permute-start.34 = (bf16[640,256]{1,0:T(8,128)(2,1)S(1)}, bf16[640,256]{1,0:T(8,128)(2,1)S(1)}, u32[]{:S(2)}, u32[]{:S(2)}) collective-permute-start(bf16[640,256]{1,0:T(8,128)(2,1)S(1)} %get-tuple-element.102), channel_id=1, source_target_pairs={{0,4},{2,6},{4,0},{6,2},{1,5},{3,7},{5,1},{7,3},{8,12},{10,14},{12... | collective-permute-start | bytes 983048 | tf_op jit(solution)/shard_map/ppermute | solution.py:20
  33.6 1.6 %collective-permute-start.35 = (bf16[640,256]{1,0:T(8,128)(2,1)S(1)}, bf16[640,256]{1,0:T(8,128)(2,1)S(1)}, u32[]{:S(2)}, u32[]{:S(2)}) collective-permute-start(bf16[640,256]{1,0:T(8,128)(2,1)S(1)} %get-tuple-element.100), channel_id=1, source_target_pairs={{0,6},{2,4},{4,2},{6,0},{1,7},{3,5},{5,3},{7,1},{8,14},{10,12},{12... | collective-permute-start | bytes 983048 | tf_op jit(solution)/shard_map/ppermute | solution.py:20
  35.2 1.4 %fusion = (s32[1,1]{1,0:T(1,128)}, s32[1,1]{1,0:T(1,128)}) fusion(s32[32,32]{1,0:T(8,128)} %param.39, s32[]{:T(128)S(6)} %select_n.31, s32[]{:T(128)S(6)} %select_n.33, s32[]{:T(128)S(6)} %select_n.34), kind=kLoop, calls=%fused_computation.14 | loop fusion | bytes 28 | tf_op jit(solution)/shard_map/dynamic_slice | solution.py:180
  38.5 5.7 %collective-permute-done.32.refs_1_ = bf16[512,256]{1,0:T(8,128)(2,1)S(1)} collective-permute-done((bf16[512,256]{1,0:T(8,128)(2,1)}, bf16[512,256]{1,0:T(8,128)(2,1)S(1)}, u32[]{:S(2)}, u32[]{:S(2)}) %collective-permute-start.32) | collective-permute-done | bytes 262176 | tf_op jit(solution)/shard_map/ppermute | solution.py:25
  44.2 1.5 %collective-permute-start.36 = (bf16[512,256]{1,0:T(8,128)(2,1)S(1)}, bf16[512,256]{1,0:T(8,128)(2,1)S(1)}, u32[]{:S(2)}, u32[]{:S(2)}) collective-permute-start(bf16[512,256]{1,0:T(8,128)(2,1)S(1)} %collective-permute-done.31.refs_0_), channel_id=1, source_target_pairs={{0,2},{2,0},{4,6},{6,4},{1,3},{3,1},{5,7},{7,5},{8,10},{10,8},{12,... | collective-permute-start | bytes 786440 | tf_op jit(solution)/shard_map/ppermute | solution.py:20
  45.7 4.5 %collective-permute-done.33 = bf16[640,256]{1,0:T(8,128)(2,1)S(1)} collective-permute-done((bf16[640,256]{1,0:T(8,128)(2,1)S(1)}, bf16[640,256]{1,0:T(8,128)(2,1)S(1)}, u32[]{:S(2)}, u32[]{:S(2)}) %collective-permute-start.33) | collective-permute-done | bytes 327712 | tf_op jit(solution)/shard_map/ppermute | solution.py:20
  50.2 7.1 %collective-permute-done.34 = bf16[640,256]{1,0:T(8,128)(2,1)S(1)} collective-permute-done((bf16[640,256]{1,0:T(8,128)(2,1)S(1)}, bf16[640,256]{1,0:T(8,128)(2,1)S(1)}, u32[]{:S(2)}, u32[]{:S(2)}) %collective-permute-start.34) | collective-permute-done | bytes 327712 | tf_op jit(solution)/shard_map/ppermute | solution.py:20
  57.2 8.9 %collective-permute-done.35 = bf16[640,256]{1,0:T(8,128)(2,1)S(1)} collective-permute-done((bf16[640,256]{1,0:T(8,128)(2,1)S(1)}, bf16[640,256]{1,0:T(8,128)(2,1)S(1)}, u32[]{:S(2)}, u32[]{:S(2)}) %collective-permute-start.35) | collective-permute-done | bytes 327712 | tf_op jit(solution)/shard_map/ppermute | solution.py:20
  66.1 3.8 %collective-permute-done.36.refs_0_ = bf16[512,256]{1,0:T(8,128)(2,1)S(1)} collective-permute-done((bf16[512,256]{1,0:T(8,128)(2,1)S(1)}, bf16[512,256]{1,0:T(8,128)(2,1)S(1)}, u32[]{:S(2)}, u32[]{:S(2)}) %collective-permute-start.36) | collective-permute-done | bytes 262176 | tf_op jit(solution)/shard_map/ppermute | solution.py:20
  71.7 2.5 %collective-permute-start.38 = (bf16[512,256]{1,0:T(8,128)(2,1)S(1)}, bf16[512,256]{1,0:T(8,128)(2,1)S(1)}, u32[]{:S(2)}, u32[]{:S(2)}) collective-permute-start(bf16[512,256]{1,0:T(8,128)(2,1)S(1)} %collective-permute-done.32.refs_1_), channel_id=1, source_target_pairs={{0,2},{2,0},{4,6},{6,4},{1,3},{3,1},{5,7},{7,5},{8,10},{10,8},{12,... | collective-permute-start | bytes 786440 | tf_op jit(solution)/shard_map/ppermute | solution.py:20
  74.4 1.7 %shard_map.133.own_ref = bf16[960,2048]{1,0:T(8,128)(2,1)S(1)} custom-call(s32[2]{0:T(128)S(1)} %pad_add_fusion.1.place_ref, bf16[4,640,256]{2,1,0:T(8,128)(2,1)S(1)} %pad_maximum_fusion.here_ref, bf16[4,640,256]{2,1,0:T(8,128)(2,1)S(1)} %collective-permute-done.37.there_ref), custom_call_target="tpu_custom_call" | custom-call | bytes 8000000 | tf_op jit(solution)/shard_map/pallas_call | solution.py:72
  76.1 2.3 %shard_map.135.refs_2_ = f32[960,512]{1,0:T(8,128)S(1)} custom-call(s32[4]{0:T(128)S(1)} %pad_add_fusion.2.order_ref, bf16[960,2048]{1,0:T(8,128)(2,1)S(1)} %shard_map.133.own_ref, bf16[512,256]{1,0:T(8,128)(2,1)S(1)} %collective-permute-done.31.refs_0_, bf16[512,256]{1,0:T(8,128)(2,1)S(1)} %collective-permute-done.32.refs_1_, ...), custom_call_target="tpu_custom_call" | custom-call | flops 1006632960 | bytes 2000000 | tf_op jit(solution)/shard_map/pallas_call | solution.py:101
  78.4 3.3 %shard_map.134.near_ref = bf16[64,2,7680]{2,1,0:T(2,128)(2,1)S(1)} custom-call(s32[9]{0:T(128)S(1)} %stack.94.order_ref, f32[2]{0:T(128)S(1)} %maximum_multiply_fusion.weight_ref, bf16[960,2048]{1,0:T(8,128)(2,1)S(1)} %shard_map.133.own_ref, bf16[4,640,256]{2,1,0:T(8,128)(2,1)S(1)} %pad_maximum_fusion.here_ref, ...), custom_call_target="tpu_custom_call" | custom-call | flops 2013265920 | bytes 4000000 | tf_op jit(solution)/shard_map/pallas_call | solution.py:127
  82.4 1.3 %shard_map.136.part_ref = f32[960,512]{1,0:T(8,128)S(1)} custom-call(s32[2]{0:T(128)S(1)} %pad_add_fusion.3.order_ref, bf16[960,2048]{1,0:T(8,128)(2,1)S(1)} %shard_map.133.own_ref, bf16[512,256]{1,0:T(8,128)(2,1)S(1)} %collective-permute-done.36.refs_0_, bf16[512,256]{1,0:T(8,128)(2,1)S(1)} %collective-permute-done.38.refs_1_, ...), custom_call_target="tpu_custom_call" | custom-call | flops 503316480 | bytes 2000000 | tf_op jit(solution)/shard_map/pallas_call | solution.py:101
  83.7 3.4 %shard_map.137 = bf16[64,2,7680]{2,1,0:T(2,128)(2,1)} custom-call(s32[3]{0:T(128)S(1)} %pad_add_fusion.order_ref, f32[2]{0:T(128)S(1)} %maximum_multiply_fusion.weight_ref, bf16[960,2048]{1,0:T(8,128)(2,1)S(1)} %shard_map.133.own_ref, bf16[64,2,7680]{2,1,0:T(2,128)(2,1)S(1)} %shard_map.134.near_ref, f32[960,512]{1,0:T(8,128)S(1)} %shard_map.136.part_ref, ...), custom_call_target="tpu_custom_call" | custom-call | flops 503316480 | bytes 6000000 | tf_op jit(solution)/shard_map/pallas_call | solution.py:157
  (23 shorter events, 5.9 us)
Async XLA Ops:
  3.3 11.3 %collective-permute-start.10 = (bf16[512,256]{1,0:T(8,128)(2,1)}, bf16[512,256]{1,0:T(8,128)(2,1)}, u32[]{:S(2)}, u32[]{:S(2)}) collective-permute-start(bf16[512,256]{1,0:T(8,128)(2,1)} %param.11), channel_id=1, source_target_pairs={{0,88},{8,80},{16,72},{24,64},{32,120},{40,112},{48,104},{56,96},{... | collective-permute-start | bytes 786440 | tf_op jit(solution)/shard_map/cond/branch_11_fun/ppermute | solution.py:20
  14.6 23.9 %collective-permute-start.31 = (bf16[512,256]{1,0:T(8,128)(2,1)}, bf16[512,256]{1,0:T(8,128)(2,1)S(1)}, u32[]{:S(2)}, u32[]{:S(2)}) collective-permute-start(bf16[512,256]{1,0:T(8,128)(2,1)} %get-tuple-element.112), channel_id=1, source_target_pairs={{0,132},{2,134},{4,128},{6,130},{8,140},{10,142},{12,136},{14,138}... | collective-permute-start | bytes 786440 | tf_op jit(solution)/shard_map/ppermute | solution.py:25
  21.4 22.8 %collective-permute-start.32 = (bf16[512,256]{1,0:T(8,128)(2,1)}, bf16[512,256]{1,0:T(8,128)(2,1)S(1)}, u32[]{:S(2)}, u32[]{:S(2)}) collective-permute-start(bf16[512,256]{1,0:T(8,128)(2,1)} %get-tuple-element.112), channel_id=1, source_target_pairs={{0,130},{2,128},{4,134},{6,132},{8,138},{10,136},{12,142},{14,140}... | collective-permute-start | bytes 786440 | tf_op jit(solution)/shard_map/ppermute | solution.py:25
  24.4 6.1 %collective-permute-start.18 = (bf16[512,256]{1,0:T(8,128)(2,1)}, bf16[512,256]{1,0:T(8,128)(2,1)}, u32[]{:S(2)}, u32[]{:S(2)}) collective-permute-start(bf16[512,256]{1,0:T(8,128)(2,1)} %param.20), channel_id=1, source_target_pairs={{0,32},{8,40},{16,48},{24,56},{32,0},{40,8},{48,16},{56,24},{64,96... | collective-permute-start | bytes 786440 | tf_op jit(solution)/shard_map/cond/branch_4_fun/ppermute | solution.py:20
  31.6 18.6 %collective-permute-start.33 = (bf16[640,256]{1,0:T(8,128)(2,1)S(1)}, bf16[640,256]{1,0:T(8,128)(2,1)S(1)}, u32[]{:S(2)}, u32[]{:S(2)}) collective-permute-start(bf16[640,256]{1,0:T(8,128)(2,1)S(1)} %get-tuple-element.101), channel_id=1, source_target_pairs={{0,2},{2,0},{4,6},{6,4},{1,3},{3,1},{5,7},{7,5},{8,10},{10,8},{12,... | collective-permute-start | bytes 983048 | tf_op jit(solution)/shard_map/ppermute | solution.py:20
  32.4 24.8 %collective-permute-start.34 = (bf16[640,256]{1,0:T(8,128)(2,1)S(1)}, bf16[640,256]{1,0:T(8,128)(2,1)S(1)}, u32[]{:S(2)}, u32[]{:S(2)}) collective-permute-start(bf16[640,256]{1,0:T(8,128)(2,1)S(1)} %get-tuple-element.102), channel_id=1, source_target_pairs={{0,4},{2,6},{4,0},{6,2},{1,5},{3,7},{5,1},{7,3},{8,12},{10,14},{12... | collective-permute-start | bytes 983048 | tf_op jit(solution)/shard_map/ppermute | solution.py:20
  33.6 32.5 %collective-permute-start.35 = (bf16[640,256]{1,0:T(8,128)(2,1)S(1)}, bf16[640,256]{1,0:T(8,128)(2,1)S(1)}, u32[]{:S(2)}, u32[]{:S(2)}) collective-permute-start(bf16[640,256]{1,0:T(8,128)(2,1)S(1)} %get-tuple-element.100), channel_id=1, source_target_pairs={{0,6},{2,4},{4,2},{6,0},{1,7},{3,5},{5,3},{7,1},{8,14},{10,12},{12... | collective-permute-start | bytes 983048 | tf_op jit(solution)/shard_map/ppermute | solution.py:20
  44.2 25.7 %collective-permute-start.36 = (bf16[512,256]{1,0:T(8,128)(2,1)S(1)}, bf16[512,256]{1,0:T(8,128)(2,1)S(1)}, u32[]{:S(2)}, u32[]{:S(2)}) collective-permute-start(bf16[512,256]{1,0:T(8,128)(2,1)S(1)} %collective-permute-done.31.refs_0_), channel_id=1, source_target_pairs={{0,2},{2,0},{4,6},{6,4},{1,3},{3,1},{5,7},{7,5},{8,10},{10,8},{12,... | collective-permute-start | bytes 786440 | tf_op jit(solution)/shard_map/ppermute | solution.py:20
  70.0 4.3 %collective-permute-start.37 = (bf16[4,640,256]{2,1,0:T(8,128)(2,1)S(1)}, bf16[4,640,256]{2,1,0:T(8,128)(2,1)S(1)}, u32[]{:S(2)}, u32[]{:S(2)}) collective-permute-start(bf16[4,640,256]{2,1,0:T(8,128)(2,1)S(1)} %pad_maximum_fusion.here_ref), channel_id=1, source_target_pairs={{0,1},{1,0},{2,3},{3,2},{4,5},{5,4},{6,7},{7,6},{8,9},{9,8},{10,11... | collective-permute-start | bytes 3932168 | tf_op jit(solution)/shard_map/ppermute | solution.py:20
  71.0 5.1 %collective-permute-start.39 = (bf16[512,256]{1,0:T(8,128)(2,1)S(1)}, bf16[512,256]{1,0:T(8,128)(2,1)}, u32[]{:S(2)}, u32[]{:S(2)}) collective-permute-start(bf16[512,256]{1,0:T(8,128)(2,1)S(1)} %collective-permute-done.31.refs_0_), channel_id=1, source_target_pairs={{0,1},{1,0},{2,3},{3,2},{4,5},{5,4},{6,7},{7,6},{8,9},{9,8},{10,11... | collective-permute-start | bytes 786440 | tf_op jit(solution)/shard_map/ppermute | solution.py:20
  71.1 5.0 %collective-permute-start.40 = (bf16[512,256]{1,0:T(8,128)(2,1)S(1)}, bf16[512,256]{1,0:T(8,128)(2,1)}, u32[]{:S(2)}, u32[]{:S(2)}) collective-permute-start(bf16[512,256]{1,0:T(8,128)(2,1)S(1)} %collective-permute-done.32.refs_1_), channel_id=1, source_target_pairs={{0,1},{1,0},{2,3},{3,2},{4,5},{5,4},{6,7},{7,6},{8,9},{9,8},{10,11... | collective-permute-start | bytes 786440 | tf_op jit(solution)/shard_map/ppermute | solution.py:20
  71.7 9.9 %collective-permute-start.38 = (bf16[512,256]{1,0:T(8,128)(2,1)S(1)}, bf16[512,256]{1,0:T(8,128)(2,1)S(1)}, u32[]{:S(2)}, u32[]{:S(2)}) collective-permute-start(bf16[512,256]{1,0:T(8,128)(2,1)S(1)} %collective-permute-done.32.refs_1_), channel_id=1, source_target_pairs={{0,2},{2,0},{4,6},{6,4},{1,3},{3,1},{5,7},{7,5},{8,10},{10,8},{12,... | collective-permute-start | bytes 786440 | tf_op jit(solution)/shard_map/ppermute | solution.py:20
  81.6 2.0 %collective-permute-start.41 = (bf16[512,256]{1,0:T(8,128)(2,1)S(1)}, bf16[512,256]{1,0:T(8,128)(2,1)S(1)}, u32[]{:S(2)}, u32[]{:S(2)}) collective-permute-start(bf16[512,256]{1,0:T(8,128)(2,1)S(1)} %collective-permute-done.36.refs_0_), channel_id=1, source_target_pairs={{0,1},{1,0},{2,3},{3,2},{4,5},{5,4},{6,7},{7,6},{8,9},{9,8},{10,11... | collective-permute-start | bytes 786440 | tf_op jit(solution)/shard_map/ppermute | solution.py:20
  82.1 1.6 %collective-permute-start.42 = (bf16[512,256]{1,0:T(8,128)(2,1)S(1)}, bf16[512,256]{1,0:T(8,128)(2,1)S(1)}, u32[]{:S(2)}, u32[]{:S(2)}) collective-permute-start(bf16[512,256]{1,0:T(8,128)(2,1)S(1)} %collective-permute-done.38.refs_1_), channel_id=1, source_target_pairs={{0,1},{1,0},{2,3},{3,2},{4,5},{5,4},{6,7},{7,6},{8,9},{9,8},{10,11... | collective-permute-start | bytes 786440 | tf_op jit(solution)/shard_map/ppermute | solution.py:20

commit v3 on v2

--- a/solution.py
+++ b/solution.py
@@ -12,7 +12,7 @@
 LAGS = 2 * LAG + 1
 TM = ("tm_0", "tm_1")
 BLK_TM = ("blk", "tm_0", "tm_1")
-GROUP = 5
+GROUP = 15
 VMEM_BYTES = 20 * 1024 * 1024
 
 def swapped(value, axis, word):

time: 87.4 us -> 87.2 us (level)
  no operation moved by 1% of the time
where the time goes in v3:
time: 87.2 us; the launch traced here: 87.1 us
  waiting for transfers between devices  41.2 us (47%)
  starting transfers between devices  24.3 us (28%)
  Pallas kernels  11.6 us (13%)
  between operations  4.59 us (5%)
  local copies, waits for them, and re-layouts  3.74 us (4%)
  other arithmetic  1.58 us (2%)
    ppermute x12, waiting for transfers between devices, swapped(): return lax.ppermute(value, axis, [(i, i ^ word) for i in range(count)])  35.1 us
    ppermute x12, starting transfers between devices, swapped(): return lax.ppermute(value, axis, [(i, i ^ word) for i in range(count)])  16.7 us
    ppermute x2, starting transfers between devices, crossed(): lax.ppermute(value, ('blk', 'tm_0'), [(i, i ^ 64 ^ word) for i in range(c...  7.62 us
    ppermute x2, waiting for transfers between devices, crossed(): lax.ppermute(value, ('blk', 'tm_0'), [(i, i ^ 64 ^ word) for i in range(c...  6.09 us
    pallas_call x2, Pallas kernels, sums(): pl.pallas_call(functools.partial(sums_kernel, count), in_specs=[smem(), v...  3.51 us
    pallas_call x1, Pallas kernels, near_round(): pl.pallas_call(near_kernel, in_specs=[smem(), smem()] + [vmem()] * 3, out...  3.26 us
    pallas_call x1, Pallas kernels, last_round(): pl.pallas_call(functools.partial(last_kernel, count), grid=(LAGS // GROUP...  3.13 us
  transfers between devices with their start and end apart: 14, of which 9 were waited for; matrix products, arithmetic and copies ran while one was open for 4% of the time, Pallas kernels for 10%

profile of v3, /device:TPU:1, one launch (start us, length us, event | category | flops | bytes accessed | tf_op | source)
XLA Modules:
  0.0 87.1 jit_solution(9291668923860896918)
XLA Ops:
  0.0 1.3 %fusion.1 = (s32[1,1]{1,0:T(1,128)}, s32[1,1]{1,0:T(1,128)}) fusion(s32[2,32]{1,0:T(2,128)} %param.38), kind=kLoop, calls=%fused_computation.15 | loop fusion | bytes 16 | tf_op jit(solution)/shard_map/slice | solution.py:176
  3.2 11.4 %conditional.3 = (bf16[512,256]{1,0:T(8,128)(2,1)}) conditional(s32[]{:T(128)} %clamp.6, bf16[512,256]{1,0:T(8,128)(2,1)} %param.37, bf16[512,256]{1,0:T(8,128)(2,1)} %param.37, bf16[512,256]{1,0:T(8,128)(2,1)} %param.37, bf16[512,256]{1,0:T(8,128)(2,1)} %param.37, bf16[512,256]{1,0:T(8,128)(2,1)} %param.37, ...), branch_computations={%region_0.1_spmd, %region_1.2_spmd, %region_2.3_spmd, %region_3.4_... | conditional | bytes 1048624 | solution.py:33
  3.3 6.1 %collective-permute-start.13 = (bf16[512,256]{1,0:T(8,128)(2,1)}, bf16[512,256]{1,0:T(8,128)(2,1)}, u32[]{:S(2)}, u32[]{:S(2)}) collective-permute-start(bf16[512,256]{1,0:T(8,128)(2,1)} %param.14), channel_id=1, source_target_pairs={{0,112},{8,120},{16,96},{24,104},{32,80},{40,88},{48,64},{56,72},{... | collective-permute-start | bytes 786440 | tf_op jit(solution)/shard_map/cond/branch_14_fun/ppermute | solution.py:20
  9.4 5.3 %collective-permute-done.13 = bf16[512,256]{1,0:T(8,128)(2,1)} collective-permute-done((bf16[512,256]{1,0:T(8,128)(2,1)}, bf16[512,256]{1,0:T(8,128)(2,1)}, u32[]{:S(2)}, u32[]{:S(2)}) %collective-permute-start.13) | collective-permute-done | bytes 262176 | tf_op jit(solution)/shard_map/cond/branch_14_fun/ppermute | solution.py:20
  14.7 6.9 %collective-permute-start.31 = (bf16[512,256]{1,0:T(8,128)(2,1)}, bf16[512,256]{1,0:T(8,128)(2,1)S(1)}, u32[]{:S(2)}, u32[]{:S(2)}) collective-permute-start(bf16[512,256]{1,0:T(8,128)(2,1)} %get-tuple-element.112), channel_id=1, source_target_pairs={{0,132},{2,134},{4,128},{6,130},{8,140},{10,142},{12,136},{14,138}... | collective-permute-start | bytes 786440 | tf_op jit(solution)/shard_map/ppermute | solution.py:25
  24.5 6.3 %conditional.4 = (bf16[512,256]{1,0:T(8,128)(2,1)}) conditional(s32[]{:T(128)} %clamp.7, bf16[512,256]{1,0:T(8,128)(2,1)} %param.37, bf16[512,256]{1,0:T(8,128)(2,1)} %param.37, bf16[512,256]{1,0:T(8,128)(2,1)} %param.37, bf16[512,256]{1,0:T(8,128)(2,1)} %param.37, bf16[512,256]{1,0:T(8,128)(2,1)} %param.37, ...), branch_computations={%region_16.17_spmd, %region_17.18_spmd, %region_18.19_spmd, %regio... | conditional | bytes 1048624 | solution.py:33
  24.6 1.0 %collective-permute-start.15 = (bf16[512,256]{1,0:T(8,128)(2,1)}, bf16[512,256]{1,0:T(8,128)(2,1)}, u32[]{:S(2)}, u32[]{:S(2)}) collective-permute-start(bf16[512,256]{1,0:T(8,128)(2,1)} %param.17), channel_id=1, source_target_pairs={{0,8},{8,0},{16,24},{24,16},{32,40},{40,32},{48,56},{56,48},{64,72... | collective-permute-start | bytes 786440 | tf_op jit(solution)/shard_map/cond/branch_1_fun/ppermute | solution.py:20
  25.6 5.2 %collective-permute-done.15 = bf16[512,256]{1,0:T(8,128)(2,1)} collective-permute-done((bf16[512,256]{1,0:T(8,128)(2,1)}, bf16[512,256]{1,0:T(8,128)(2,1)}, u32[]{:S(2)}, u32[]{:S(2)}) %collective-permute-start.15) | collective-permute-done | bytes 262176 | tf_op jit(solution)/shard_map/cond/branch_1_fun/ppermute | solution.py:20
  30.8 1.0 %pad_maximum_fusion.4 = (bf16[640,256]{1,0:T(8,128)(2,1)S(1)}, bf16[640,256]{1,0:T(8,128)(2,1)S(1)}, bf16[640,256]{1,0:T(8,128)(2,1)S(1)}, bf16[640,256]{1,0:T(8,128)(2,1)S(1)}) fusion(bf16[128,256]{1,0:T(8,128)(2,1)S(1)} %get-tuple-element.104, bf16[512,256]{1,0:T(8,128)(2,1)} %get-tuple-element.114, bf16[128,256]{1,0:T(8,128)(2,1)S(1)} %get-tuple-element.106, ...), kind=kLoop, calls=%fused_computation.4 | loop fusion | flops 2129920 | bytes 1835008 | tf_op jit(solution)/shard_map/concatenate | solution.py:200
  32.7 1.2 %collective-permute-start.34 = (bf16[640,256]{1,0:T(8,128)(2,1)S(1)}, bf16[640,256]{1,0:T(8,128)(2,1)S(1)}, u32[]{:S(2)}, u32[]{:S(2)}) collective-permute-start(bf16[640,256]{1,0:T(8,128)(2,1)S(1)} %get-tuple-element.102), channel_id=1, source_target_pairs={{0,4},{2,6},{4,0},{6,2},{1,5},{3,7},{5,1},{7,3},{8,12},{10,14},{12... | collective-permute-start | bytes 983048 | tf_op jit(solution)/shard_map/ppermute | solution.py:20
  33.9 1.6 %collective-permute-start.35 = (bf16[640,256]{1,0:T(8,128)(2,1)S(1)}, bf16[640,256]{1,0:T(8,128)(2,1)S(1)}, u32[]{:S(2)}, u32[]{:S(2)}) collective-permute-start(bf16[640,256]{1,0:T(8,128)(2,1)S(1)} %get-tuple-element.100), channel_id=1, source_target_pairs={{0,6},{2,4},{4,2},{6,0},{1,7},{3,5},{5,3},{7,1},{8,14},{10,12},{12... | collective-permute-start | bytes 983048 | tf_op jit(solution)/shard_map/ppermute | solution.py:20
  35.5 1.4 %fusion = (s32[1,1]{1,0:T(1,128)}, s32[1,1]{1,0:T(1,128)}) fusion(s32[32,32]{1,0:T(8,128)} %param.39, s32[]{:T(128)S(6)} %select_n.31, s32[]{:T(128)S(6)} %select_n.33, s32[]{:T(128)S(6)} %select_n.34), kind=kLoop, calls=%fused_computation.14 | loop fusion | bytes 28 | tf_op jit(solution)/shard_map/dynamic_slice | solution.py:180
  38.7 5.7 %collective-permute-done.32.refs_1_ = bf16[512,256]{1,0:T(8,128)(2,1)S(1)} collective-permute-done((bf16[512,256]{1,0:T(8,128)(2,1)}, bf16[512,256]{1,0:T(8,128)(2,1)S(1)}, u32[]{:S(2)}, u32[]{:S(2)}) %collective-permute-start.32) | collective-permute-done | bytes 262176 | tf_op jit(solution)/shard_map/ppermute | solution.py:25
  44.3 1.5 %collective-permute-start.36 = (bf16[512,256]{1,0:T(8,128)(2,1)S(1)}, bf16[512,256]{1,0:T(8,128)(2,1)S(1)}, u32[]{:S(2)}, u32[]{:S(2)}) collective-permute-start(bf16[512,256]{1,0:T(8,128)(2,1)S(1)} %collective-permute-done.31.refs_0_), channel_id=1, source_target_pairs={{0,2},{2,0},{4,6},{6,4},{1,3},{3,1},{5,7},{7,5},{8,10},{10,8},{12,... | collective-permute-start | bytes 786440 | tf_op jit(solution)/shard_map/ppermute | solution.py:20
  45.9 4.7 %collective-permute-done.33 = bf16[640,256]{1,0:T(8,128)(2,1)S(1)} collective-permute-done((bf16[640,256]{1,0:T(8,128)(2,1)S(1)}, bf16[640,256]{1,0:T(8,128)(2,1)S(1)}, u32[]{:S(2)}, u32[]{:S(2)}) %collective-permute-start.33) | collective-permute-done | bytes 327712 | tf_op jit(solution)/shard_map/ppermute | solution.py:20
  50.6 7.1 %collective-permute-done.34 = bf16[640,256]{1,0:T(8,128)(2,1)S(1)} collective-permute-done((bf16[640,256]{1,0:T(8,128)(2,1)S(1)}, bf16[640,256]{1,0:T(8,128)(2,1)S(1)}, u32[]{:S(2)}, u32[]{:S(2)}) %collective-permute-start.34) | collective-permute-done | bytes 327712 | tf_op jit(solution)/shard_map/ppermute | solution.py:20
  57.7 8.8 %collective-permute-done.35 = bf16[640,256]{1,0:T(8,128)(2,1)S(1)} collective-permute-done((bf16[640,256]{1,0:T(8,128)(2,1)S(1)}, bf16[640,256]{1,0:T(8,128)(2,1)S(1)}, u32[]{:S(2)}, u32[]{:S(2)}) %collective-permute-start.35) | collective-permute-done | bytes 327712 | tf_op jit(solution)/shard_map/ppermute | solution.py:20
  66.5 3.8 %collective-permute-done.36.refs_0_ = bf16[512,256]{1,0:T(8,128)(2,1)S(1)} collective-permute-done((bf16[512,256]{1,0:T(8,128)(2,1)S(1)}, bf16[512,256]{1,0:T(8,128)(2,1)S(1)}, u32[]{:S(2)}, u32[]{:S(2)}) %collective-permute-start.36) | collective-permute-done | bytes 262176 | tf_op jit(solution)/shard_map/ppermute | solution.py:20
  72.0 2.5 %collective-permute-start.38 = (bf16[512,256]{1,0:T(8,128)(2,1)S(1)}, bf16[512,256]{1,0:T(8,128)(2,1)S(1)}, u32[]{:S(2)}, u32[]{:S(2)}) collective-permute-start(bf16[512,256]{1,0:T(8,128)(2,1)S(1)} %collective-permute-done.32.refs_1_), channel_id=1, source_target_pairs={{0,2},{2,0},{4,6},{6,4},{1,3},{3,1},{5,7},{7,5},{8,10},{10,8},{12,... | collective-permute-start | bytes 786440 | tf_op jit(solution)/shard_map/ppermute | solution.py:20
  74.7 1.7 %shard_map.133.own_ref = bf16[960,2048]{1,0:T(8,128)(2,1)S(1)} custom-call(s32[2]{0:T(128)S(1)} %pad_add_fusion.1.place_ref, bf16[4,640,256]{2,1,0:T(8,128)(2,1)S(1)} %pad_maximum_fusion.here_ref, bf16[4,640,256]{2,1,0:T(8,128)(2,1)S(1)} %collective-permute-done.37.there_ref), custom_call_target="tpu_custom_call" | custom-call | bytes 8000000 | tf_op jit(solution)/shard_map/pallas_call | solution.py:72
  76.4 2.3 %shard_map.135.refs_2_ = f32[960,512]{1,0:T(8,128)S(1)} custom-call(s32[4]{0:T(128)S(1)} %pad_add_fusion.2.order_ref, bf16[960,2048]{1,0:T(8,128)(2,1)S(1)} %shard_map.133.own_ref, bf16[512,256]{1,0:T(8,128)(2,1)S(1)} %collective-permute-done.31.refs_0_, bf16[512,256]{1,0:T(8,128)(2,1)S(1)} %collective-permute-done.32.refs_1_, ...), custom_call_target="tpu_custom_call" | custom-call | flops 1006632960 | bytes 2000000 | tf_op jit(solution)/shard_map/pallas_call | solution.py:101
  78.6 3.3 %shard_map.134.near_ref = bf16[64,2,7680]{2,1,0:T(2,128)(2,1)S(1)} custom-call(s32[9]{0:T(128)S(1)} %stack.94.order_ref, f32[2]{0:T(128)S(1)} %maximum_multiply_fusion.weight_ref, bf16[960,2048]{1,0:T(8,128)(2,1)S(1)} %shard_map.133.own_ref, bf16[4,640,256]{2,1,0:T(8,128)(2,1)S(1)} %pad_maximum_fusion.here_ref, ...), custom_call_target="tpu_custom_call" | custom-call | flops 2013265920 | bytes 4000000 | tf_op jit(solution)/shard_map/pallas_call | solution.py:127
  82.7 1.3 %shard_map.136.part_ref = f32[960,512]{1,0:T(8,128)S(1)} custom-call(s32[2]{0:T(128)S(1)} %pad_add_fusion.3.order_ref, bf16[960,2048]{1,0:T(8,128)(2,1)S(1)} %shard_map.133.own_ref, bf16[512,256]{1,0:T(8,128)(2,1)S(1)} %collective-permute-done.36.refs_0_, bf16[512,256]{1,0:T(8,128)(2,1)S(1)} %collective-permute-done.38.refs_1_, ...), custom_call_target="tpu_custom_call" | custom-call | flops 503316480 | bytes 2000000 | tf_op jit(solution)/shard_map/pallas_call | solution.py:101
  83.9 3.1 %shard_map.137 = bf16[64,2,7680]{2,1,0:T(2,128)(2,1)} custom-call(s32[3]{0:T(128)S(1)} %pad_add_fusion.order_ref, f32[2]{0:T(128)S(1)} %maximum_multiply_fusion.weight_ref, bf16[960,2048]{1,0:T(8,128)(2,1)S(1)} %shard_map.133.own_ref, bf16[64,2,7680]{2,1,0:T(2,128)(2,1)S(1)} %shard_map.134.near_ref, f32[960,512]{1,0:T(8,128)S(1)} %shard_map.136.part_ref, ...), custom_call_target="tpu_custom_call" | custom-call | flops 503316480 | bytes 6000000 | tf_op jit(solution)/shard_map/pallas_call | solution.py:157
  (23 shorter events, 5.6 us)
Async XLA Ops:
  3.3 11.4 %collective-permute-start.13 = (bf16[512,256]{1,0:T(8,128)(2,1)}, bf16[512,256]{1,0:T(8,128)(2,1)}, u32[]{:S(2)}, u32[]{:S(2)}) collective-permute-start(bf16[512,256]{1,0:T(8,128)(2,1)} %param.14), channel_id=1, source_target_pairs={{0,112},{8,120},{16,96},{24,104},{32,80},{40,88},{48,64},{56,72},{... | collective-permute-start | bytes 786440 | tf_op jit(solution)/shard_map/cond/branch_14_fun/ppermute | solution.py:20
  14.7 24.0 %collective-permute-start.31 = (bf16[512,256]{1,0:T(8,128)(2,1)}, bf16[512,256]{1,0:T(8,128)(2,1)S(1)}, u32[]{:S(2)}, u32[]{:S(2)}) collective-permute-start(bf16[512,256]{1,0:T(8,128)(2,1)} %get-tuple-element.112), channel_id=1, source_target_pairs={{0,132},{2,134},{4,128},{6,130},{8,140},{10,142},{12,136},{14,138}... | collective-permute-start | bytes 786440 | tf_op jit(solution)/shard_map/ppermute | solution.py:25
  21.6 22.8 %collective-permute-start.32 = (bf16[512,256]{1,0:T(8,128)(2,1)}, bf16[512,256]{1,0:T(8,128)(2,1)S(1)}, u32[]{:S(2)}, u32[]{:S(2)}) collective-permute-start(bf16[512,256]{1,0:T(8,128)(2,1)} %get-tuple-element.112), channel_id=1, source_target_pairs={{0,130},{2,128},{4,134},{6,132},{8,138},{10,136},{12,142},{14,140}... | collective-permute-start | bytes 786440 | tf_op jit(solution)/shard_map/ppermute | solution.py:25
  24.6 6.2 %collective-permute-start.15 = (bf16[512,256]{1,0:T(8,128)(2,1)}, bf16[512,256]{1,0:T(8,128)(2,1)}, u32[]{:S(2)}, u32[]{:S(2)}) collective-permute-start(bf16[512,256]{1,0:T(8,128)(2,1)} %param.17), channel_id=1, source_target_pairs={{0,8},{8,0},{16,24},{24,16},{32,40},{40,32},{48,56},{56,48},{64,72... | collective-permute-start | bytes 786440 | tf_op jit(solution)/shard_map/cond/branch_1_fun/ppermute | solution.py:20
  31.8 18.8 %collective-permute-start.33 = (bf16[640,256]{1,0:T(8,128)(2,1)S(1)}, bf16[640,256]{1,0:T(8,128)(2,1)S(1)}, u32[]{:S(2)}, u32[]{:S(2)}) collective-permute-start(bf16[640,256]{1,0:T(8,128)(2,1)S(1)} %get-tuple-element.101), channel_id=1, source_target_pairs={{0,2},{2,0},{4,6},{6,4},{1,3},{3,1},{5,7},{7,5},{8,10},{10,8},{12,... | collective-permute-start | bytes 983048 | tf_op jit(solution)/shard_map/ppermute | solution.py:20
  32.7 25.0 %collective-permute-start.34 = (bf16[640,256]{1,0:T(8,128)(2,1)S(1)}, bf16[640,256]{1,0:T(8,128)(2,1)S(1)}, u32[]{:S(2)}, u32[]{:S(2)}) collective-permute-start(bf16[640,256]{1,0:T(8,128)(2,1)S(1)} %get-tuple-element.102), channel_id=1, source_target_pairs={{0,4},{2,6},{4,0},{6,2},{1,5},{3,7},{5,1},{7,3},{8,12},{10,14},{12... | collective-permute-start | bytes 983048 | tf_op jit(solution)/shard_map/ppermute | solution.py:20
  33.9 32.6 %collective-permute-start.35 = (bf16[640,256]{1,0:T(8,128)(2,1)S(1)}, bf16[640,256]{1,0:T(8,128)(2,1)S(1)}, u32[]{:S(2)}, u32[]{:S(2)}) collective-permute-start(bf16[640,256]{1,0:T(8,128)(2,1)S(1)} %get-tuple-element.100), channel_id=1, source_target_pairs={{0,6},{2,4},{4,2},{6,0},{1,7},{3,5},{5,3},{7,1},{8,14},{10,12},{12... | collective-permute-start | bytes 983048 | tf_op jit(solution)/shard_map/ppermute | solution.py:20
  44.3 26.0 %collective-permute-start.36 = (bf16[512,256]{1,0:T(8,128)(2,1)S(1)}, bf16[512,256]{1,0:T(8,128)(2,1)S(1)}, u32[]{:S(2)}, u32[]{:S(2)}) collective-permute-start(bf16[512,256]{1,0:T(8,128)(2,1)S(1)} %collective-permute-done.31.refs_0_), channel_id=1, source_target_pairs={{0,2},{2,0},{4,6},{6,4},{1,3},{3,1},{5,7},{7,5},{8,10},{10,8},{12,... | collective-permute-start | bytes 786440 | tf_op jit(solution)/shard_map/ppermute | solution.py:20
  70.5 4.2 %collective-permute-start.37 = (bf16[4,640,256]{2,1,0:T(8,128)(2,1)S(1)}, bf16[4,640,256]{2,1,0:T(8,128)(2,1)S(1)}, u32[]{:S(2)}, u32[]{:S(2)}) collective-permute-start(bf16[4,640,256]{2,1,0:T(8,128)(2,1)S(1)} %pad_maximum_fusion.here_ref), channel_id=1, source_target_pairs={{0,1},{1,0},{2,3},{3,2},{4,5},{5,4},{6,7},{7,6},{8,9},{9,8},{10,11... | collective-permute-start | bytes 3932168 | tf_op jit(solution)/shard_map/ppermute | solution.py:20
  71.2 5.1 %collective-permute-start.39 = (bf16[512,256]{1,0:T(8,128)(2,1)S(1)}, bf16[512,256]{1,0:T(8,128)(2,1)}, u32[]{:S(2)}, u32[]{:S(2)}) collective-permute-start(bf16[512,256]{1,0:T(8,128)(2,1)S(1)} %collective-permute-done.31.refs_0_), channel_id=1, source_target_pairs={{0,1},{1,0},{2,3},{3,2},{4,5},{5,4},{6,7},{7,6},{8,9},{9,8},{10,11... | collective-permute-start | bytes 786440 | tf_op jit(solution)/shard_map/ppermute | solution.py:20
  71.3 5.0 %collective-permute-start.40 = (bf16[512,256]{1,0:T(8,128)(2,1)S(1)}, bf16[512,256]{1,0:T(8,128)(2,1)}, u32[]{:S(2)}, u32[]{:S(2)}) collective-permute-start(bf16[512,256]{1,0:T(8,128)(2,1)S(1)} %collective-permute-done.32.refs_1_), channel_id=1, source_target_pairs={{0,1},{1,0},{2,3},{3,2},{4,5},{5,4},{6,7},{7,6},{8,9},{9,8},{10,11... | collective-permute-start | bytes 786440 | tf_op jit(solution)/shard_map/ppermute | solution.py:20
  72.0 9.9 %collective-permute-start.38 = (bf16[512,256]{1,0:T(8,128)(2,1)S(1)}, bf16[512,256]{1,0:T(8,128)(2,1)S(1)}, u32[]{:S(2)}, u32[]{:S(2)}) collective-permute-start(bf16[512,256]{1,0:T(8,128)(2,1)S(1)} %collective-permute-done.32.refs_1_), channel_id=1, source_target_pairs={{0,2},{2,0},{4,6},{6,4},{1,3},{3,1},{5,7},{7,5},{8,10},{10,8},{12,... | collective-permute-start | bytes 786440 | tf_op jit(solution)/shard_map/ppermute | solution.py:20
  81.9 2.0 %collective-permute-start.41 = (bf16[512,256]{1,0:T(8,128)(2,1)S(1)}, bf16[512,256]{1,0:T(8,128)(2,1)S(1)}, u32[]{:S(2)}, u32[]{:S(2)}) collective-permute-start(bf16[512,256]{1,0:T(8,128)(2,1)S(1)} %collective-permute-done.36.refs_0_), channel_id=1, source_target_pairs={{0,1},{1,0},{2,3},{3,2},{4,5},{5,4},{6,7},{7,6},{8,9},{9,8},{10,11... | collective-permute-start | bytes 786440 | tf_op jit(solution)/shard_map/ppermute | solution.py:20
  82.4 1.6 %collective-permute-start.42 = (bf16[512,256]{1,0:T(8,128)(2,1)S(1)}, bf16[512,256]{1,0:T(8,128)(2,1)S(1)}, u32[]{:S(2)}, u32[]{:S(2)}) collective-permute-start(bf16[512,256]{1,0:T(8,128)(2,1)S(1)} %collective-permute-done.38.refs_1_), channel_id=1, source_target_pairs={{0,1},{1,0},{2,3},{3,2},{4,5},{5,4},{6,7},{7,6},{8,9},{9,8},{10,11... | collective-permute-start | bytes 786440 | tf_op jit(solution)/shard_map/ppermute | solution.py:20
